TPU v7x, 128 devices: a whole 4x4x4 slice. The times are simulated.
128 devices in a mesh: seq: 16 (over x, y), ep: 8 (over z, core).
Axes of the slice: x: 4, y: 4, z: 4, core: 2. Of those that a mesh axis runs over, the one named last changes fastest.
Arguments:
- latent_cache: bfloat16 [128, 16384, 576], P('ep', 'seq'), may hold values from -6 to 6
- queries: bfloat16 [128, 128, 576], P('ep', 'seq'), may hold values from -12 to 12
- lengths: int32 [128], P('ep'), may hold values from 2 to 16384, as said below
- up_value: bfloat16 [128, 512, 128], P(('seq', 'ep')), may hold values from -1.1953125 to 1.1953125
- out_proj: bfloat16 [128, 128, 7168], P(('seq', 'ep')), may hold values from -0.1875 to 0.1875
- residual: bfloat16 [128, 7168], P(('seq', 'ep')), may hold values from -10 to 10
- norm_gain: bfloat16 [7168], replicated, may hold values from 0.099609375 to 1.8984375
- routes: int32 [128, 8], P(('seq', 'ep')), may hold values from 0 to 15, all different within a row
- route_weight: float32 [128, 8], P(('seq', 'ep')), may hold values from 0.1 to 1
- expert_gate: bfloat16 [16, 7168, 1024], P('seq', None, 'ep'), may hold values from -0.0625 to 0.0625
- expert_up: bfloat16 [16, 7168, 1024], P('seq', None, 'ep'), may hold values from -0.0625 to 0.0625
- expert_down: bfloat16 [16, 1024, 7168], P('seq', 'ep'), may hold values from -0.1875 to 0.1875
Outputs:
- mixed: bfloat16 [128, 7168], P(('seq', 'ep'))
Inputs may be any that keep to these rules, and one draw needn't show every extreme that they name: `lengths`: some sequence uses all 16384 positions. `routes`: each row names 8 different experts.
All inputs are finite; a program needn't handle non-finite values.
Results may differ from a plain program's by a relative error of at most 0.035.
Values may be sent and summed in bfloat16 or wider, within the bound.
A program may use at most 128 MiB of HBM per device.

v0:
```python
import jax
import jax.numpy as jnp
from jax import lax
from jax.sharding import PartitionSpec as P

LAT = 512
BLK = 512


score_scale = 192.0 ** (-0.5)
masked_score = -1e30


def merge_groups(partials):
    summed, row_tops, row_totals = partials
    global_top = jnp.max(row_tops, axis=0)
    factor = jnp.exp(row_tops - global_top[None])
    numerator = jnp.sum(summed * factor[..., None], axis=0)
    denominator = jnp.sum(row_totals * factor, axis=0)
    return (numerator / denominator[..., None]).astype(jnp.bfloat16)


def attend(queries, latent_cache, lengths):
    all_heads = lax.all_gather(queries, "seq", axis=1, tiled=True)
    seq_rows = all_heads.shape[0]
    head_count = all_heads.shape[1]
    local_span = latent_cache.shape[1]
    offset = lax.axis_index("seq") * local_span

    def one_block(carry, block_index):
        row_top, row_total, summed = carry
        block_start = block_index * BLK
        key_block = lax.dynamic_slice_in_dim(latent_cache, block_start, BLK, 1)
        scores = (
            jnp.einsum("bhk,btk->hbt", all_heads, key_block, preferred_element_type=jnp.float32)
            * score_scale
        )
        position = offset + block_start + jnp.arange(BLK, dtype=jnp.int32)
        is_live = (position[None, :] < lengths[:, None])[None]
        scores = jnp.where(is_live, scores, masked_score)
        block_top = jnp.max(scores, axis=2)
        exp_scores = jnp.where(is_live, jnp.exp(scores - block_top[..., None]), 0.0)
        block_total = jnp.sum(exp_scores, axis=2)
        rounded = exp_scores.astype(jnp.bfloat16)
        block_sum = jnp.einsum(
            "hbt,btl->hbl", rounded, key_block[:, :, :LAT], preferred_element_type=jnp.float32
        )
        new_top = jnp.maximum(row_top, block_top)
        old_weight = jnp.exp(row_top - new_top)
        new_weight = jnp.exp(block_top - new_top)
        row_total = row_total * old_weight + block_total * new_weight
        summed = summed * old_weight[..., None] + block_sum * new_weight[..., None]
        return ((new_top, row_total, summed), None)

    initial = (
        jnp.full((head_count, seq_rows), masked_score, jnp.float32),
        jnp.zeros((head_count, seq_rows), jnp.float32),
        jnp.zeros((head_count, seq_rows, LAT), jnp.float32),
    )
    finals, _ = lax.scan(one_block, initial, jnp.arange(local_span // BLK, dtype=jnp.int32))
    return finals


def shards(
    latent_cache,
    queries,
    lengths,
    up_value,
    out_proj,
    residual,
    norm_gain,
    routes,
    route_weight,
    expert_gate,
    expert_up,
    expert_down,
):
    row_tops, row_totals, summed = attend(queries, latent_cache, lengths)
    partials = (summed[None], row_tops[None], row_totals[None])
    gathered = (
        lax.all_to_all(
            lax.all_to_all(
                partials[0].astype(jnp.bfloat16), "seq", split_axis=1, concat_axis=0, tiled=True
            ),
            "ep",
            split_axis=1,
            concat_axis=2,
            tiled=True,
        ).astype(jnp.float32),
        lax.all_to_all(
            lax.all_to_all(
                partials[1].astype(jnp.bfloat16), "seq", split_axis=1, concat_axis=0, tiled=True
            ),
            "ep",
            split_axis=1,
            concat_axis=2,
            tiled=True,
        ).astype(jnp.float32),
        lax.all_to_all(
            lax.all_to_all(
                partials[2].astype(jnp.bfloat16), "seq", split_axis=1, concat_axis=0, tiled=True
            ),
            "ep",
            split_axis=1,
            concat_axis=2,
            tiled=True,
        ).astype(jnp.float32),
    )
    latent_out = merge_groups(gathered)
    head_values = jnp.einsum(
        "hsl,hlv->hsv", latent_out, up_value, preferred_element_type=jnp.float32
    ).astype(jnp.bfloat16)
    own_rows = residual.shape[0]
    model_width = residual.shape[1]
    attended = lax.psum_scatter(
        jnp.einsum("hsv,hvd->sd", head_values, out_proj, preferred_element_type=jnp.float32),
        ("seq", "ep"),
        scatter_dimension=0,
        tiled=True,
    )
    hidden = (residual.astype(jnp.float32) + attended).astype(jnp.bfloat16)
    hidden_float = hidden.astype(jnp.float32)
    rms_scale = lax.rsqrt(jnp.mean(hidden_float * hidden_float, axis=1, keepdims=True) + 1e-06)
    normed = (hidden_float * rms_scale * norm_gain.astype(jnp.float32)[None, :]).astype(
        jnp.bfloat16
    )
    seq_count = lax.axis_size("seq")
    ep_count = lax.axis_size("ep")
    local_experts = expert_gate.shape[0]
    experts_all = seq_count * local_experts
    matches = (
        routes[:, :, None] == jnp.arange(experts_all, dtype=jnp.int32)[None, None, :]
    ).astype(jnp.float32)
    weights = jnp.sum(route_weight[:, :, None] * matches, axis=1)
    chosen = jnp.sum(matches, axis=1)
    marked = chosen.T.reshape(seq_count, 1, local_experts, own_rows)
    marked = jnp.broadcast_to(marked, (seq_count, ep_count, local_experts, own_rows)).reshape(
        seq_count * ep_count, local_experts, own_rows
    )
    outgoing = marked[..., None].astype(jnp.bfloat16) * normed[None, None]
    incoming = lax.all_to_all(outgoing, ("seq", "ep"), split_axis=0, concat_axis=0, tiled=True)
    sources = incoming.shape[0]
    item_count = incoming.shape[2]
    flat_rows = incoming[:, 0].reshape(sources * item_count, model_width)
    gate_pre = jnp.dot(flat_rows, expert_gate[0], preferred_element_type=jnp.float32)
    up_proj = jnp.dot(flat_rows, expert_up[0], preferred_element_type=jnp.float32)
    active = (jax.nn.silu(gate_pre) * up_proj).astype(jnp.bfloat16)
    output = jnp.dot(active, expert_down[0], preferred_element_type=jnp.float32)
    results = [output.reshape(sources, item_count, model_width)]
    stacked = jnp.stack(results, axis=1)
    came_back = lax.all_to_all(
        stacked.astype(jnp.bfloat16), ("seq", "ep"), split_axis=0, concat_axis=0, tiled=True
    ).astype(stacked.dtype)
    per_expert = came_back.reshape(seq_count, ep_count, local_experts, own_rows, model_width).sum(
        axis=1
    )
    per_expert = per_expert.reshape(experts_all, own_rows, model_width)
    combined = jnp.einsum("re,erd->rd", weights, per_expert)
    return (hidden_float + combined).astype(jnp.bfloat16)


def solution(mesh):
    placed = (
        P("ep", "seq", None),
        P("ep", "seq", None),
        P("ep"),
        P(("seq", "ep"), None, None),
        P(("seq", "ep"), None, None),
        P(("seq", "ep"), None),
        P(),
        P(("seq", "ep"), None),
        P(("seq", "ep"), None),
        P("seq", None, "ep"),
        P("seq", None, "ep"),
        P("seq", "ep", None),
    )
    return jax.shard_map(
        shards, mesh=mesh, in_specs=placed, out_specs=P(("seq", "ep"), None), check_vma=False
    )
```

profile of v0, /device:TPU:1, one launch (start us, length us, event | category | flops | bytes accessed | tf_op | source)
XLA Modules:
  0.0 524.9 jit_solution(13885434471836599193)
XLA Ops:
  6.5 1.7 copy.41
  8.3 0.0 all-gather.2.cloned.1.call-update
  8.3 50.2 %all-gather.2.cloned.1.call-done = bf16[16,128,576]{2,0,1:T(8,128)(2,1)} async-done(((bf16[16,8,576]{2,0,1:T(8,128)(2,1)}), bf16[16,128,576]{2,0,1:T(8,128)(2,1)}) %all-gather.2.cloned.1.call-update) | async-done | bytes 2359312 | tf_op jit(solution)/shard_map/all_gather | solution.py:24
  58.6 4.7 copy.42
  63.3 44.4 %while.15 = (s32[]{:T(128)}, f32[128,16]{0,1:T(8,128)S(1)}, f32[128,16]{0,1:T(8,128)S(1)}, f32[128,16,512]{0,2,1:T(8,128)}, s32[2]{0:T(128)S(1)}, /*index=5*/s32...) while((s32[]{:T(128)}, f32[128,16]{0,1:T(8,128)S(1)}, ...), condition=%wide.region_3.4_spmd.clone, body=%wide.region_0.3_spmd.clone.sunk | while | flops 2299548160 | bytes 58093884 | solution.py:60
  63.3 0.6 dynamic_slice.16
  64.5 0.1 broadcast_compare_fusion.2
  64.6 7.2 %bitcast_reduce_fusion.4 = (f32[128,16]{0,1:T(8,128)S(1)}, f32[16,512,128]{2,1,0:T(8,128)S(1)}) fusion(pred[16,512]{1,0:T(8,128)(4,1)S(1)} %broadcast_compare_fusion.2, bf16[16,128,576]{1,2,0:T(8,128)(2,1)} %get-tuple-element.245, bf16[16,1024,576]{1,2,0:T(8,128)(2,1)} %get-tuple-element.244, s32[]{:T(128)S(6)} %select_n.44), kind=kOutput, calls=%fused_computation.7.clone.1 | convolution fusion | flops 1211103232 | bytes 16007172 | tf_op jit(solution)/shard_map/while/body/eval_jaxpr/bhk,btk->hbt/dot_general | solution.py:35
  71.8 2.0 copy-done.1
  73.7 2.8 fusion.76
  76.6 8.4 %fusion.78 = f32[128,16,512]{0,2,1:T(8,128)} fusion(f32[128,16,512]{0,2,1:T(8,128)} %get-tuple-element.227, bf16[16,1024,576]{1,2,0:T(8,128)(2,1)} %get-tuple-element.244, s32[]{:T(128)S(6)} %select_n.44, f32[16,512,128]{2,1,0:T(8,128)} %copy-done.1, f32[128,16]{0,1:T(8,128)S(1)} %get-tuple-element.209, f32[128,16]{0,1:T(8,128)S(1)} %get-tuple-element.210, ...), kind=kOutput, calls=%fused_computation.5.clone.1 | convolution fusion | flops 1083179008 | bytes 21012484 | tf_op jit(solution)/shard_map/while/body/eval_jaxpr/hbt,btl->hbl/dot_general | solution.py:45
  85.0 0.6 dynamic_slice.16
  86.2 0.1 broadcast_compare_fusion.2
  86.3 7.2 %bitcast_reduce_fusion.4 = (f32[128,16]{0,1:T(8,128)S(1)}, f32[16,512,128]{2,1,0:T(8,128)S(1)}) fusion(pred[16,512]{1,0:T(8,128)(4,1)S(1)} %broadcast_compare_fusion.2, bf16[16,128,576]{1,2,0:T(8,128)(2,1)} %get-tuple-element.245, bf16[16,1024,576]{1,2,0:T(8,128)(2,1)} %get-tuple-element.244, s32[]{:T(128)S(6)} %select_n.44), kind=kOutput, calls=%fused_computation.7.clone.1 | convolution fusion | flops 1211103232 | bytes 16007172 | tf_op jit(solution)/shard_map/while/body/eval_jaxpr/bhk,btk->hbt/dot_general | solution.py:35
  93.5 2.0 copy-done.1
  95.5 2.8 fusion.76
  98.4 9.4 %fusion.78 = f32[128,16,512]{0,2,1:T(8,128)} fusion(f32[128,16,512]{0,2,1:T(8,128)} %get-tuple-element.227, bf16[16,1024,576]{1,2,0:T(8,128)(2,1)} %get-tuple-element.244, s32[]{:T(128)S(6)} %select_n.44, f32[16,512,128]{2,1,0:T(8,128)} %copy-done.1, f32[128,16]{0,1:T(8,128)S(1)} %get-tuple-element.209, f32[128,16]{0,1:T(8,128)S(1)} %get-tuple-element.210, ...), kind=kOutput, calls=%fused_computation.5.clone.1 | convolution fusion | flops 1083179008 | bytes 21012484 | tf_op jit(solution)/shard_map/while/body/eval_jaxpr/hbt,btl->hbl/dot_general | solution.py:45
  107.7 0.8 copy.45
  108.5 4.1 all-to-all-start.2
  112.6 0.7 copy.47
  113.3 5.8 %all-to-all-done.2 = bf16[1,128,16]{2,0,1:T(2,128)(2,1)S(1)} async-done(((bf16[1,128,16]{2,0,1:T(2,128)(2,1)}), bf16[1,128,16]{2,0,1:T(2,128)(2,1)S(1)}, u32[]{:S(2)}, u32[]{:S(2)}) %all-to-all-start.2) | async-done | bytes 4128 | tf_op jit(solution)/shard_map/all_to_all | solution.py:91
  119.1 3.5 all-to-all-start.4
  122.6 0.7 reshape.399
  123.3 5.7 %all-to-all-done.4 = bf16[1,128,16]{2,0,1:T(2,128)(2,1)S(1)} async-done(((bf16[1,128,16]{2,0,1:T(2,128)(2,1)}), bf16[1,128,16]{2,0,1:T(2,128)(2,1)S(1)}, u32[]{:S(2)}, u32[]{:S(2)}) %all-to-all-start.4) | async-done | bytes 4128 | tf_op jit(solution)/shard_map/all_to_all | solution.py:100
  129.0 8.6 %all-to-all-start.3 = ((bf16[8,2,128]{2,1,0:T(2,128)(2,1)}), bf16[8,2,128]{2,1,0:T(2,128)(2,1)S(1)}, u32[]{:S(2)}, u32[]{:S(2)}) async-start(bf16[8,2,128]{2,1,0:T(2,128)(2,1)} %reshape.399), calls=%async_computation.3 | async-start | bytes 8192 | tf_op jit(solution)/shard_map/all_to_all | solution.py:90
  137.6 5.1 copy.43
  142.7 4.4 all-to-all-start
  147.2 0.7 reshape.401
  147.9 28.7 %all-to-all-done = bf16[1,128,16,512]{3,2,0,1:T(8,128)(2,1)} async-done(((bf16[1,128,16,512]{3,2,0,1:T(8,128)(2,1)}), bf16[1,128,16,512]{3,2,0,1:T(8,128)(2,1)}, u32[]{:S(2)}, u32[]{:S(2)}) %all-to-all-start) | async-done | bytes 2097184 | tf_op jit(solution)/shard_map/all_to_all | solution.py:82
  176.6 6.0 %all-to-all-start.5 = ((bf16[8,2,128]{2,1,0:T(2,128)(2,1)}), bf16[8,2,128]{2,1,0:T(2,128)(2,1)S(1)}, u32[]{:S(2)}, u32[]{:S(2)}) async-start(bf16[8,2,128]{2,1,0:T(2,128)(2,1)} %reshape.401), calls=%async_computation.5 | async-start | bytes 8192 | tf_op jit(solution)/shard_map/all_to_all | solution.py:99
  182.6 3.1 copy.44
  185.8 1.4 all-to-all-done.5
  187.1 4.9 all-to-all-start.1
  192.1 0.1 reshape.400
  192.2 0.1 reshape.402
  192.3 26.2 %all-to-all-done.1 = bf16[16,8,16,512]{3,2,0,1:T(8,128)(2,1)} async-done(((bf16[16,8,16,512]{3,2,0,1:T(8,128)(2,1)}), bf16[16,8,16,512]{3,2,0,1:T(8,128)(2,1)}, u32[]{:S(2)}, u32[]{:S(2)}) %all-to-all-start.1) | async-done | bytes 2097184 | tf_op jit(solution)/shard_map/all_to_all | solution.py:81
  218.5 2.1 multiply_reduce_fusion
  220.6 0.1 divide_convert_fusion
  220.7 0.0 copy-start.4
  220.7 0.0 copy-start.6
  220.7 0.0 copy-start.7
  220.8 2.6 fusion.33
  223.4 0.0 all-reduce.3.cloned.1.call-update
  223.5 0.1 select_reduce_fusion
  223.5 0.1 broadcast_in_dim.60
  223.6 0.1 convert_element_type.136
  223.7 150.8 %all-reduce.3.cloned.1.call-done = f32[128,7168]{1,0:T(8,128)} async-done(((f32[128,7168]{1,0:T(8,128)}), f32[128,7168]{1,0:T(8,128)}) %all-reduce.3.cloned.1.call-update) | async-done | bytes 3670032
  374.5 1.6 multiply_reduce_fusion.2
  376.8 0.1 convert_reduce_fusion
  376.9 4.5 broadcast_multiply_fusion
  381.4 0.5 broadcast.228
  381.9 13.1 %reduce.19 = bf16[128,7168]{1,0:T(8,128)(2,1)} reduce(bf16[128,1,1,7168]{3,2,1,0:T(2,128)(2,1)} %broadcast_multiply_fusion, bf16[]{:T(256)} %broadcast.228), dimensions={1,2}, to_apply=%broadcast_multiply_fusion.reduce_sub_computation | reduce | bytes 3670018 | tf_op jit(solution)/shard_map/mul | solution.py:140
  395.0 5.4 %reshape.403 = bf16[128,2,3584]{2,1,0:T(2,128)(2,1)} reshape(bf16[128,7168]{1,0:T(8,128)(2,1)} %reduce.19) | data formatting | bytes 3670016
  400.4 34.4 %all_to_all.73 = bf16[128,2,3584]{2,1,0:T(2,128)(2,1)} all-to-all(bf16[128,2,3584]{2,1,0:T(2,128)(2,1)} %reshape.403), channel_id=1, replica_groups=mesh['seq'=16,'ep'=8] {'seq','ep'}, dimensions={0} | all-to-all | bytes 3670016 | tf_op jit(solution)/shard_map/all_to_all | solution.py:141
  434.8 11.5 %reshape.404 = bf16[128,1,1,7168]{3,2,1,0:T(2,128)(2,1)} reshape(bf16[128,2,3584]{2,1,0:T(2,128)(2,1)} %all_to_all.73) | data formatting | bytes 3670016
  446.3 3.5 fusion.28
  449.8 5.8 %fusion.24 = bf16[128,1,1,7168]{3,0,2,1:T(8,128)(2,1)} fusion(bf16[1,128,7168]{2,1,0:T(8,128)(2,1)} %param.25, bf16[1,7168,128]{2,1,0:T(8,128)(2,1)} %param.24, bf16[128,1,1,7168]{3,2,1,0:T(2,128)(2,1)} %reshape.404, f32[128,128]{1,0:T(8,128)S(1)} %fusion.28), kind=kOutput, calls=%fused_computation.33 | convolution fusion | flops 470777856 | bytes 7405568 | tf_op jit(solution)/shard_map/dot_general | solution.py:148
  455.6 4.2 reduce.20
  459.8 5.4 %reshape.405 = bf16[128,2,3584]{2,1,0:T(2,128)(2,1)} reshape(bf16[128,7168]{1,0:T(8,128)(2,1)} %reduce.20) | data formatting | bytes 3670016
  465.2 33.4 %all_to_all.74 = bf16[128,2,3584]{2,1,0:T(2,128)(2,1)} all-to-all(bf16[128,2,3584]{2,1,0:T(2,128)(2,1)} %reshape.405), channel_id=1, replica_groups=mesh['seq'=16,'ep'=8] {'seq','ep'}, dimensions={0} | all-to-all | bytes 3670016 | tf_op jit(solution)/shard_map/all_to_all | solution.py:151
  498.6 11.5 %reshape.406 = bf16[128,1,1,7168]{3,2,1,0:T(2,128)(2,1)} reshape(bf16[128,2,3584]{2,1,0:T(2,128)(2,1)} %all_to_all.74) | data formatting | bytes 3670016
  510.0 5.8 %reshape.394 = f32[128,1,1,7168]{3,2,1,0:T(1,128)S(1)} convert(bf16[128,1,1,7168]{3,2,1,0:T(2,128)(2,1)} %reshape.406) | non-fusion elementwise | flops 917504 | bytes 5505024 | tf_op jit(solution)/shard_map/reshape | solution.py:154
  515.9 1.5 bitcast_reduce_fusion.1
  517.3 0.8 fusion.25
  (34 shorter events, 0.2 us)
Async XLA Ops:
  6.5 214.2 %copy-start = (bf16[1,128,7168]{2,1,0:T(8,128)(2,1)S(1)}, bf16[1,128,7168]{2,1,0:T(8,128)(2,1)}, u32[]{:S(2)}) copy-start(bf16[1,128,7168]{2,1,0:T(8,128)(2,1)} %param.18) | copy-start | bytes 5505028
  6.5 56.7 %copy-start.5 = (s32[16]{0:T(128)S(1)}, s32[16]{0:T(128)}, u32[]{:S(2)}) copy-start(s32[16]{0:T(128)} %param.16) | copy-start | bytes 196
  6.5 52.0 %all-gather.2.cloned.1.call-start = ((), (), s32[]{:S(2)}) async-start(), calls=%async_computation.8 | async-start | bytes 2785280 | tf_op jit(solution)/shard_map/all_gather | solution.py:24
  71.8 2.0 copy-start.1
  93.5 2.0 copy-start.1
  108.5 10.6 %all-to-all-start.2 = ((bf16[1,128,16]{2,0,1:T(2,128)(2,1)}), bf16[1,128,16]{2,0,1:T(2,128)(2,1)S(1)}, u32[]{:S(2)}, u32[]{:S(2)}) async-start(bf16[1,128,16]{2,0,1:T(2,128)(2,1)} %copy.45), calls=%async_computation.2 | async-start | bytes 131072 | tf_op jit(solution)/shard_map/all_to_all | solution.py:91
  119.1 10.0 %all-to-all-start.4 = ((bf16[1,128,16]{2,0,1:T(2,128)(2,1)}), bf16[1,128,16]{2,0,1:T(2,128)(2,1)S(1)}, u32[]{:S(2)}, u32[]{:S(2)}) async-start(bf16[1,128,16]{2,0,1:T(2,128)(2,1)} %copy.47), calls=%async_computation.4 | async-start | bytes 131072 | tf_op jit(solution)/shard_map/all_to_all | solution.py:100
  129.0 13.7 %all-to-all-start.3 = ((bf16[8,2,128]{2,1,0:T(2,128)(2,1)}), bf16[8,2,128]{2,1,0:T(2,128)(2,1)S(1)}, u32[]{:S(2)}, u32[]{:S(2)}) async-start(bf16[8,2,128]{2,1,0:T(2,128)(2,1)} %reshape.399), calls=%async_computation.3 | async-start | bytes 8192 | tf_op jit(solution)/shard_map/all_to_all | solution.py:90
  142.7 33.9 %all-to-all-start = ((bf16[1,128,16,512]{3,2,0,1:T(8,128)(2,1)}), bf16[1,128,16,512]{3,2,0,1:T(8,128)(2,1)}, u32[]{:S(2)}, u32[]{:S(2)}) async-start(bf16[1,128,16,512]{3,2,0,1:T(8,128)(2,1)} %bitcast.102), calls=%async_computation | async-start | bytes 4194304 | tf_op jit(solution)/shard_map/all_to_all | solution.py:82
  176.6 10.5 %all-to-all-start.5 = ((bf16[8,2,128]{2,1,0:T(2,128)(2,1)}), bf16[8,2,128]{2,1,0:T(2,128)(2,1)S(1)}, u32[]{:S(2)}, u32[]{:S(2)}) async-start(bf16[8,2,128]{2,1,0:T(2,128)(2,1)} %reshape.401), calls=%async_computation.5 | async-start | bytes 8192 | tf_op jit(solution)/shard_map/all_to_all | solution.py:99
  185.8 34.9 %copy-start.2 = (bf16[1,512,128]{2,1,0:T(8,128)(2,1)S(1)}, bf16[1,512,128]{2,1,0:T(8,128)(2,1)}, u32[]{:S(2)}) copy-start(bf16[1,512,128]{2,1,0:T(8,128)(2,1)} %param.17) | copy-start | bytes 393220
  187.1 31.4 %all-to-all-start.1 = ((bf16[16,8,16,512]{3,2,0,1:T(8,128)(2,1)}), bf16[16,8,16,512]{3,2,0,1:T(8,128)(2,1)}, u32[]{:S(2)}, u32[]{:S(2)}) async-start(bf16[16,8,16,512]{3,2,0,1:T(8,128)(2,1)} %copy.44), calls=%async_computation.1 | async-start | bytes 4194304 | tf_op jit(solution)/shard_map/all_to_all | solution.py:81
  192.1 182.5 %all-reduce.3.cloned.1.call-start = ((), (), s32[]{:S(2)}) async-start(), calls=%async_computation.9 | async-start | bytes 7340032
  220.7 2.7 copy-start.4
  220.7 2.7 copy-start.6
  220.7 2.7 copy-start.7
  220.8 153.8 %copy-start.3 = (bf16[1,7168]{1,0:T(2,128)(2,1)S(1)}, bf16[1,7168]{1,0:T(2,128)(2,1)}, u32[]{:S(2)}) copy-start(bf16[1,7168]{1,0:T(2,128)(2,1)} %param.19) | copy-start | bytes 43012
Sparse Core Ops, SparseCore 0:
  9.5 48.9 all-gather.1
  223.5 150.9 all-reduce.2
where the time goes:
time: 527 us; the launch traced here: 525 us
  waiting for transfers between devices  269 us (51%)
  blocking collectives  67.8 us (13%)
  local copies, waits for them, and re-layouts  57.3 us (11%)
  matrix products  44.8 us (9%)
  other arithmetic  39 us (7%)
  starting transfers between devices  31.5 us (6%)
  between operations  14.4 us (3%)
    unnamed x3, waiting for transfers between devices  151 us
    all_gather x1, waiting for transfers between devices, attend(): all_heads = lax.all_gather(queries, 'seq', axis=1, tiled=True)  50.2 us
    unnamed x26, local copies, waits for them, and re-layouts  41.7 us
    all_to_all x1, blocking collectives, shards(): lax.all_to_all(outgoing, ('seq', 'ep'), split_axis=0, concat_axis=0, tile...  34.4 us
    all_to_all x1, blocking collectives, shards(): lax.all_to_all(stacked.astype(jnp.bfloat16), ('seq', 'ep'), split_axis=0,...  33.4 us
    all_to_all x1, waiting for transfers between devices, shards(): lax.all_to_all(partials[0].astype(jnp.bfloat16), 'seq', split_axis=1, con...  28.7 us
    all_to_all x1, waiting for transfers between devices, shards(): lax.all_to_all(lax.all_to_all(partials[0].astype(jnp.bfloat16), 'seq', sp...  26.2 us
    dot_general x2, matrix products, one_block(): jnp.einsum('hbt,btl->hbl', rounded, key_block[:, :, :LAT], preferred_elem...  17.7 us
  transfers between devices with their start and end apart: 8, of which 7 were waited for; matrix products, arithmetic and copies ran while one was open for 2% of the time, Pallas kernels for 0%

commit v1 on v0

v1 whole, which is shorter than its diff:
```python
import functools
import math

import jax
import jax.numpy as jnp
from jax import lax
from jax.experimental import pallas as pl
from jax.experimental.pallas import tpu as pltpu
from jax.sharding import PartitionSpec as P

MESH = pl.DeviceIdType.MESH
F32 = jnp.float32
BF16 = jnp.bfloat16
masked_score = -1e30
PAIR = 2
EXTRA = 128
WEIGHT_LANE = 16


def three_parts(value):
    high = value.astype(BF16).astype(F32)
    rest = value - high
    middle = rest.astype(BF16).astype(F32)
    return high, middle, (rest - middle).astype(BF16).astype(F32)


def drain(ref, sem):
    pltpu.make_async_copy(ref, ref, sem).wait()


def decode_kernel(
    side, ep, scale, width,
    lens, routes, route_w, cache, q, upv, outp, res, gain, gate, upw, down,
    out,
    kbuf, qg, obuf, st_own, st_got, lat, r1, r2_own, r2, latent,
    upg, opr, edr, gu, hv, r5_own, r5, resg, hid, u1, upl, usb, act, r8_own, r8, mix_own, mix_got,
    k_sem, own_sem, a1_s, a1_r, a2_s, a2_r, st_s, st_r, r1_s, r1_r, r2_s, r2_r,
    w_s, w_r, x_s, x_r, p_s, p_r, c_s, c_r,
):
    seq = side * side
    batch, span, _ = kbuf.shape
    chunks = batch // PAIR
    heads, lat_dim = obuf.shape[1:]
    group = heads // seq
    vdim = upv.shape[2]
    cols = opr.shape[2]
    units = gate.shape[2]
    half = ep // 2
    quarter = ep // 4
    rows_all = seq * ep

    s_me = lax.axis_index("seq")
    e_me = lax.axis_index("ep")
    x, y = lax.div(s_me, side), lax.rem(s_me, side)
    core = lax.rem(e_me, 2)
    sibling = e_me + 1 - 2 * core

    def axes(parity):
        return x + parity * (y - x), y + parity * (x - y)

    def plane(parity, a, b):
        return (a * side + b) + parity * ((b * side + a) - (a * side + b))

    def send(src, dst, send_sem, recv_sem, s, e):
        pltpu.make_async_remote_copy(
            src_ref=src, dst_ref=dst, send_sem=send_sem, recv_sem=recv_sem,
            device_id=(s, e), device_id_type=MESH,
        ).start()

    def each(lo, hi, body):
        lax.fori_loop(lo, hi, lambda i, c: (body(i), c)[1], 0)

    def other_seq(d):
        return lax.rem(s_me + d, seq)

    def other_ep(d):
        return lax.rem(e_me + d, ep)

    barrier = pltpu.get_barrier_semaphore()
    each(1, seq, lambda d: pl.semaphore_signal(
        barrier, inc=1, device_id=(other_seq(d), e_me), device_id_type=MESH))
    each(1, ep, lambda d: pl.semaphore_signal(
        barrier, inc=1, device_id=(s_me, other_ep(d)), device_id_type=MESH))

    def own_query(c):
        a, b = axes(lax.rem(c, 2))
        return pltpu.make_async_copy(
            q.at[pl.ds(c * PAIR, PAIR)], qg.at[c, a, b], own_sem.at[c])

    def load_cache(i):
        return pltpu.make_async_copy(cache.at[i], kbuf.at[i], k_sem.at[i])

    own_weights = [
        pltpu.make_async_copy(upv.at[0], upg.at[:, pl.ds(pl.multiple_of(e_me * vdim, vdim), vdim)], own_sem.at[chunks]),
        pltpu.make_async_copy(outp.at[0, :, pl.ds(pl.multiple_of(e_me * cols, cols), cols)], opr.at[e_me], own_sem.at[chunks + 1]),
        pltpu.make_async_copy(down.at[0, :, pl.ds(pl.multiple_of(e_me * cols, cols), cols)], edr.at[e_me], own_sem.at[chunks + 2]),
        pltpu.make_async_copy(gate.at[0], gu.at[:, pl.ds(0, units)], own_sem.at[chunks + 3]),
        pltpu.make_async_copy(upw.at[0], gu.at[:, pl.ds(units, units)], own_sem.at[chunks + 4]),
    ]
    each(0, chunks, lambda c: own_query(c).start())
    each(0, batch, lambda i: load_cache(i).start())
    for copy in own_weights:
        copy.start()
    resg[e_me] = res[e_me]

    pl.semaphore_wait(barrier, seq - 1 + ep - 1)

    def gather_first(c):
        parity = lax.rem(c, 2)
        a, b = axes(parity)
        for d in range(1, side):
            send(q.at[pl.ds(c * PAIR, PAIR)], qg.at[c, a, b], a1_s.at[c], a1_r.at[c],
                 plane(parity, lax.rem(a + d, side), b), e_me)

    each(0, chunks, gather_first)

    def spread(d):
        e = other_ep(d)
        here = pl.ds(pl.multiple_of(e * cols, cols), cols)
        send(upv.at[0], upg.at[:, pl.ds(pl.multiple_of(e_me * vdim, vdim), vdim)], w_s.at[0], w_r.at[0], s_me, e)
        send(outp.at[0, :, here], opr.at[e_me], w_s.at[1], w_r.at[1], s_me, e)
        send(res.at[e], resg.at[e_me], w_s.at[3], w_r.at[3], s_me, e)

    def spread_down(d):
        e = other_ep(d)
        here = pl.ds(pl.multiple_of(e * cols, cols), cols)
        send(down.at[0, :, here], edr.at[e_me], w_s.at[2], w_r.at[2], s_me, e)

    each(1, ep, spread)
    each(1, ep, spread_down)

    def gather_second(c):
        parity = lax.rem(c, 2)
        a, b = axes(parity)
        own_query(c).wait()
        drain(qg.at[c, pl.ds(0, side - 1), 0], a1_r.at[c])
        for d in range(1, side):
            send(qg.at[c, :, b], qg.at[c, :, b], a2_s.at[c], a2_r.at[c],
                 plane(parity, a, lax.rem(b + d, side)), e_me)

    eye = lax.broadcasted_iota(jnp.int32, (heads, heads), 0) == lax.broadcasted_iota(jnp.int32, (heads, heads), 1)

    def to_row(column):
        return jnp.sum(jnp.where(eye, column, 0.0), axis=0, keepdims=True)

    def to_column(row):
        return jnp.sum(jnp.where(eye, row, 0.0), axis=1, keepdims=True)

    position = s_me * span + lax.broadcasted_iota(jnp.int32, (1, span), 1)

    def attend(c):
        drain(qg.at[c, pl.ds(0, side - 1)], a2_r.at[c])
        for j in range(PAIR):
            i = c * PAIR + j
            load_cache(i).wait()
            queries = qg[c, :, :, j].astype(F32).reshape(heads, -1).astype(BF16)
            scores = lax.dot_general(queries, kbuf[i], (((1,), (1,)), ((), ())), preferred_element_type=F32)
            live = position < lens[i]
            scores = jnp.where(live, scores, masked_score)
            top = jnp.max(scores, axis=1, keepdims=True)
            prob = jnp.where(live, jnp.exp2((scores - top) * (scale * math.log2(math.e))), 0.0)
            total = jnp.sum(prob, axis=1, keepdims=True)
            obuf[i] = jnp.dot(prob.astype(BF16), kbuf[i, :, :lat_dim], preferred_element_type=F32)
            st_own[c, j:j + 1] = to_row(top)
            st_own[c, PAIR + j:PAIR + j + 1] = to_row(total)
        each(1, seq, lambda d: send(
            st_own.at[c], st_got.at[c, d - 1], st_s.at[c], st_r.at[c], other_seq(d), e_me))

    def scale_own(c):
        parity = lax.rem(c, 2)
        a, b = axes(parity)
        drain(st_got.at[c], st_r.at[c])
        own = st_own[c]
        got = st_got[c]
        own_top, own_total = own[:PAIR], own[PAIR:]
        tops, totals = got[:, :PAIR], got[:, PAIR:]
        top = jnp.maximum(own_top, jnp.max(tops, axis=0))
        own_factor = jnp.exp((own_top - top) * scale)
        den = own_total * own_factor + jnp.sum(totals * jnp.exp((tops - top[None]) * scale), axis=0)
        factor = own_factor / den
        for j in range(PAIR):
            scaled = obuf[c * PAIR + j] * to_column(factor[j:j + 1])
            lat[c, :, j] = scaled.reshape(side, side * group, lat_dim).astype(BF16)
        for d in range(1, side):
            to = lax.rem(a + d, side)
            send(lat.at[c, to], r1.at[c, d - 1], r1_s.at[c], r1_r.at[c], plane(parity, to, b), e_me)

    def sum_first(c):
        parity = lax.rem(c, 2)
        a, b = axes(parity)
        drain(r1.at[c], r1_r.at[c])
        for j in range(PAIR):
            total = lat[c, a, j].astype(F32)
            for d in range(side - 1):
                total += r1[c, d, j].astype(F32)
            r2_own[c, :, j] = total.reshape(side, group, lat_dim).astype(BF16)
        for d in range(1, side):
            to = lax.rem(b + d, side)
            send(r2_own.at[c, to], r2.at[c, d - 1], r2_s.at[c], r2_r.at[c], plane(parity, a, to), e_me)

    def sum_second(c):
        a, b = axes(lax.rem(c, 2))
        drain(r2.at[c], r2_r.at[c])
        total = r2_own[c, b].astype(F32)
        for d in range(side - 1):
            total += r2[c, d].astype(F32)
        latent[pl.ds(c * PAIR, PAIR)] = total

    ahead = 2
    each(0, min(ahead, chunks), gather_second)

    def stage(i):
        pl.when(i < chunks)(lambda: attend(i))
        pl.when(i + ahead < chunks)(lambda: gather_second(i + ahead))
        pl.when(jnp.logical_and(i >= 1, i < chunks + 1))(lambda: scale_own(i - 1))
        pl.when(jnp.logical_and(i >= 2, i < chunks + 2))(lambda: sum_first(i - 2))
        pl.when(i >= 3)(lambda: sum_second(i - 3))

    each(0, chunks + 3, stage)

    own_weights[0].wait()
    drain(upg.at[:, pl.ds(0, (ep - 1) * vdim)], w_r.at[0])
    latents = latent[...].reshape(batch * group, lat_dim).astype(BF16)
    values = jnp.dot(latents, upg[...], preferred_element_type=F32)
    row = lax.broadcasted_iota(jnp.int32, values.shape, 0)
    column = lax.broadcasted_iota(jnp.int32, values.shape, 1)
    values = jnp.where(lax.rem(row, group) == lax.div(column, vdim), values, 0.0)
    hv[e_me] = jnp.sum(values.reshape(batch, group, group * vdim), axis=1).astype(BF16)
    each(1, ep, lambda d: send(hv.at[e_me], hv.at[e_me], x_s.at[0], x_r.at[0], s_me, other_ep(d)))

    own_weights[1].wait()
    drain(opr.at[pl.ds(0, ep - 1)], w_r.at[1])
    drain(hv.at[pl.ds(0, ep - 1)], x_r.at[0])
    attended = jnp.dot(
        hv[...].reshape(rows_all, group * vdim), opr[...].reshape(ep * vdim, cols), preferred_element_type=F32)
    r5_own[...] = attended.reshape(seq, ep, cols).astype(BF16)
    each(1, seq, lambda d: send(
        r5_own.at[other_seq(d)], r5.at[d - 1], x_s.at[1], x_r.at[1], other_seq(d), e_me))

    drain(resg.at[pl.ds(0, ep - 1)], w_r.at[3])
    residual = resg[...].reshape(ep, cols)
    lane = lax.broadcasted_iota(jnp.int32, (ep, EXTRA), 1)
    sub = lax.broadcasted_iota(jnp.int32, (ep, EXTRA), 0)
    expert = lax.div(lane - WEIGHT_LANE, 3)
    part = lax.rem(lane - WEIGHT_LANE, 3)
    weight = jnp.zeros((ep, EXTRA), F32)
    for k in range(routes.shape[1]):
        weight += jnp.where(expert == routes[0, k], route_w[0, k], 0.0)
    w_high, w_mid, w_low = three_parts(weight)
    weight = jnp.where(part == 0, w_high, jnp.where(part == 1, w_mid, w_low))
    weight = jnp.where(jnp.logical_and(sub == e_me, lane >= WEIGHT_LANE), weight, 0.0)

    drain(r5, x_r.at[1])
    hidden = r5_own[s_me].astype(F32)
    for d in range(seq - 1):
        hidden += r5[d].astype(F32)
    hidden = (hidden + residual).astype(BF16).astype(F32)
    hid[...] = hidden
    s_high, s_mid, s_low = three_parts(jnp.sum(hidden * hidden, axis=1, keepdims=True))
    squares = jnp.where(lane == 0, s_high, jnp.where(lane == 1, s_mid, jnp.where(lane == 2, s_low, 0.0)))
    u1[e_me, :, :cols] = (hidden * gain[e_me]).astype(BF16)
    u1[e_me, :, cols:] = (squares + weight).astype(BF16)
    each(1, ep, lambda d: send(u1.at[e_me], u1.at[e_me], x_s.at[2], x_r.at[2], s_me, other_ep(d)))

    drain(u1.at[pl.ds(0, ep - 1)], x_r.at[2])
    for t in range(2):
        a, b = axes(t)
        upl[t, a, b] = u1[pl.ds(core * half + t * quarter, quarter)]
        for d in range(1, side):
            send(upl.at[t, a, b], upl.at[t, a, b], p_s.at[t], p_r.at[t], plane(t, lax.rem(a + d, side), b), e_me)
    for t in range(2):
        a, b = axes(t)
        drain(upl.at[t, pl.ds(0, side - 1), 0], p_r.at[t])
        for d in range(1, side):
            send(upl.at[t, :, b], upl.at[t, :, b], p_s.at[2 + t], p_r.at[2 + t], plane(t, a, lax.rem(b + d, side)), e_me)
    for t in range(2):
        drain(upl.at[t, pl.ds(0, side - 1)], p_r.at[2 + t])
        send(upl.at[t], usb.at[t], c_s.at[t], c_r.at[t], s_me, sibling)

    own_weights[3].wait()
    own_weights[4].wait()
    gated = jnp.zeros((rows_all, 2 * units), F32)
    extra = jnp.zeros((rows_all, EXTRA), F32)
    for which in range(2):
        for t in range(2):
            buf = (upl, usb)[which]
            if which:
                drain(usb.at[t], c_r.at[t])
            first = (core + which * (1 - 2 * core)) * half + t * quarter
            for k in range(quarter):
                rows = [
                    (buf[t, i, j, k] if t == 0 else buf[t, j, i, k]).astype(F32)
                    for i in range(side) for j in range(side)
                ]
                rows = jnp.concatenate(rows, axis=0)
                at = pl.ds(pl.multiple_of((first + k) * cols, cols), cols)
                gated += jnp.dot(rows[:, :cols].astype(BF16), gu[at, :], preferred_element_type=F32)
                extra += rows[:, cols:]

    lane = lax.broadcasted_iota(jnp.int32, extra.shape, 1)
    mine = WEIGHT_LANE + 3 * s_me
    squares = jnp.sum(jnp.where(lane < 3, extra, 0.0), axis=1, keepdims=True)
    weight = jnp.sum(jnp.where(jnp.logical_and(lane >= mine, lane < mine + 3), extra, 0.0), axis=1, keepdims=True)
    rms = lax.rsqrt(squares / width + 1e-6)
    gated = gated * rms
    gate_pre, up_pre = gated[:, :units], gated[:, units:]
    act[e_me] = (gate_pre / (1.0 + jnp.exp(-gate_pre)) * up_pre).astype(BF16)
    each(1, ep, lambda d: send(act.at[e_me], act.at[e_me], x_s.at[3], x_r.at[3], s_me, other_ep(d)))

    own_weights[2].wait()
    drain(edr.at[pl.ds(0, ep - 1)], w_r.at[2])
    drain(act.at[pl.ds(0, ep - 1)], x_r.at[3])
    acts = jnp.concatenate([act[e] for e in range(ep)], axis=1)
    result = jnp.dot(acts, edr[...].reshape(ep * units, cols), preferred_element_type=F32) * weight
    r8_own[...] = result.reshape(seq, ep, cols).astype(BF16)
    each(1, seq, lambda d: send(
        r8_own.at[other_seq(d)], r8.at[d - 1], x_s.at[4], x_r.at[4], other_seq(d), e_me))

    drain(r8, x_r.at[4])
    mixed = r8_own[s_me].astype(F32)
    for d in range(seq - 1):
        mixed += r8[d].astype(F32)
    mixed = mixed + hid[...]
    mix_own[...] = mixed.reshape(ep, 1, cols)
    mix_got[e_me] = mix_own[e_me]
    each(1, ep, lambda d: send(
        mix_own.at[other_ep(d)], mix_got.at[e_me], x_s.at[5], x_r.at[5], s_me, other_ep(d)))
    drain(mix_got.at[pl.ds(0, ep - 1)], x_r.at[5])
    out[...] = mix_got[...]

    def sent(c):
        drain(qg.at[c, pl.ds(0, side - 1), 0], a1_s.at[c])
        drain(qg.at[c, pl.ds(0, side - 1)], a2_s.at[c])
        drain(st_got.at[c], st_s.at[c])
        drain(r1.at[c], r1_s.at[c])
        drain(r2.at[c], r2_s.at[c])

    each(0, chunks, sent)
    drain(upg.at[:, pl.ds(0, (ep - 1) * vdim)], w_s.at[0])
    drain(opr.at[pl.ds(0, ep - 1)], w_s.at[1])
    drain(edr.at[pl.ds(0, ep - 1)], w_s.at[2])
    drain(resg.at[pl.ds(0, ep - 1)], w_s.at[3])
    drain(hv.at[pl.ds(0, ep - 1)], x_s.at[0])
    drain(r5, x_s.at[1])
    drain(u1.at[pl.ds(0, ep - 1)], x_s.at[2])
    drain(act.at[pl.ds(0, ep - 1)], x_s.at[3])
    drain(r8, x_s.at[4])
    drain(mix_got.at[pl.ds(0, ep - 1)], x_s.at[5])
    for t in range(2):
        drain(upl.at[t, pl.ds(0, side - 1), 0], p_s.at[t])
        drain(upl.at[t, pl.ds(0, side - 1)], p_s.at[2 + t])
        drain(usb.at[t], c_s.at[t])


def shards(
    seq, ep, latent_cache, queries, lengths, up_value, out_proj, residual, norm_gain,
    routes, route_weight, expert_gate, expert_up, expert_down,
):
    side = math.isqrt(seq)
    batch, span, kdim = latent_cache.shape
    group = queries.shape[1]
    heads = group * seq
    lat_dim, vdim = up_value.shape[1:]
    width = residual.shape[1]
    cols = width // ep
    units = expert_gate.shape[2]
    chunks = batch // PAIR
    rows_all = seq * ep
    dma = pltpu.SemaphoreType.DMA
    vmem = pltpu.VMEM
    scratch = [
        vmem((batch, span, kdim), BF16),
        vmem((chunks, side, side, PAIR, group, kdim), BF16),
        vmem((batch, heads, lat_dim), F32),
        vmem((chunks, 2 * PAIR, heads), F32),
        vmem((chunks, seq - 1, 2 * PAIR, heads), F32),
        vmem((chunks, side, PAIR, side * group, lat_dim), BF16),
        vmem((chunks, side - 1, PAIR, side * group, lat_dim), BF16),
        vmem((chunks, side, PAIR, group, lat_dim), BF16),
        vmem((chunks, side - 1, PAIR, group, lat_dim), BF16),
        vmem((batch, group, lat_dim), F32),
        vmem((lat_dim, ep * vdim), BF16),
        vmem((ep, vdim, cols), BF16),
        vmem((ep, units, cols), BF16),
        vmem((width, 2 * units), BF16),
        vmem((ep, batch, group * vdim), BF16),
        vmem((seq, ep, cols), BF16),
        vmem((seq - 1, ep, cols), BF16),
        vmem((ep, 1, cols), F32),
        vmem((ep, cols), F32),
        vmem((ep, ep, cols + EXTRA), BF16),
        vmem((2, side, side, ep // 4, ep, cols + EXTRA), BF16),
        vmem((2, side, side, ep // 4, ep, cols + EXTRA), BF16),
        vmem((ep, rows_all, units), BF16),
        vmem((seq, ep, cols), BF16),
        vmem((seq - 1, ep, cols), BF16),
        vmem((ep, 1, cols), F32),
        vmem((ep, 1, cols), F32),
        dma((batch,)),
        dma((chunks + 5,)),
    ]
    scratch += [dma((chunks,)) for _ in range(10)]
    scratch += [dma((4,)), dma((4,)), dma((6,)), dma((6,)), dma((4,)), dma((4,)), dma((2,)), dma((2,))]
    smem = pl.BlockSpec(memory_space=pltpu.SMEM)
    whole = pl.BlockSpec(memory_space=pltpu.VMEM)
    anywhere = pl.BlockSpec(memory_space=pl.ANY)
    mixed = pl.pallas_call(
        functools.partial(decode_kernel, side, ep, 192.0 ** (-0.5), width),
        out_shape=jax.ShapeDtypeStruct((ep, 1, cols), F32),
        in_specs=[smem, smem, smem] + [anywhere] * 4 + [whole, whole] + [anywhere] * 3,
        out_specs=whole,
        scratch_shapes=scratch,
        compiler_params=pltpu.CompilerParams(
            collective_id=0, has_side_effects=True, vmem_limit_bytes=58 * 1024 * 1024),
        name="decode",
    )(
        lengths, routes, route_weight, latent_cache, queries, up_value, out_proj,
        residual.astype(F32).reshape(ep, 1, cols), norm_gain.astype(F32).reshape(ep, 1, cols),
        expert_gate, expert_up, expert_down,
    )
    return mixed.reshape(1, width).astype(BF16)


def solution(mesh):
    placed = (
        P("ep", "seq", None),
        P("ep", "seq", None),
        P("ep"),
        P(("seq", "ep"), None, None),
        P(("seq", "ep"), None, None),
        P(("seq", "ep"), None),
        P(),
        P(("seq", "ep"), None),
        P(("seq", "ep"), None),
        P("seq", None, "ep"),
        P("seq", None, "ep"),
        P("seq", "ep", None),
    )
    return jax.shard_map(
        functools.partial(shards, mesh.shape["seq"], mesh.shape["ep"]),
        mesh=mesh, in_specs=placed, out_specs=P(("seq", "ep"), None), check_vma=False,
    )
```

time: 527 us -> 149 us (0.28)
  waiting for transfers between devices: 269 us -> 0 us
  Pallas kernels: 0 us -> 118 us
  blocking collectives: 67.8 us -> 0 us
  matrix products: 44.8 us -> 0 us
  other arithmetic: 39 us -> 4.08 us
  starting transfers between devices: 31.5 us -> 0 us
  local copies, waits for them, and re-layouts: 57.3 us -> 26.6 us
  between operations: 14.4 us -> 0.01 us
    unnamed x3 -> x0, waiting for transfers between devices: 151 us -> none
    pallas_call x0 -> x1, Pallas kernels: none -> 118 us  [shards(): pl.pallas_call(functools.partial(decode_kernel, side, ep, 192.0 ** (-0.5)...]
    all_to_all x6 -> x0, waiting for transfers between devices: 67.8 us -> none  [the longest x1 28.7 us: shards(): lax.all_to_all(partials[0].astype(jnp.bfloat16), 'seq', split_axis=1, con...]
    all_to_all x2 -> x0, blocking collectives: 67.8 us -> none  [the longest x1 34.4 us: shards(): lax.all_to_all(outgoing, ('seq', 'ep'), split_axis=0, concat_axis=0, tile...]
    all_gather x1 -> x0, waiting for transfers between devices: 50.2 us -> none  [attend(): all_heads = lax.all_gather(queries, 'seq', axis=1, tiled=True)]
    dot_general x8 -> x0, matrix products: 44.8 us -> none  [the longest x2 17.7 us: one_block(): jnp.einsum('hbt,btl->hbl', rounded, key_block[:, :, :LAT], preferred_elem...]
    all_to_all x6 -> x0, starting transfers between devices: 31.5 us -> none  [the longest x1 8.59 us: shards(): lax.all_to_all(lax.all_to_all(partials[1].astype(jnp.bfloat16), 'seq', sp...]
    mul x2 -> x0, other arithmetic: 17.6 us -> none  [shards(): outgoing = marked[..., None].astype(jnp.bfloat16) * normed[None, None]]
  transfers between devices with their start and end apart: 8 -> 0, of which waited for: 7 -> 0; matrix products, arithmetic and copies ran while one was open for 2% -> 0% of each run, Pallas kernels for 0% -> 0%
where the time goes in v1:
time: 149 us; the launch traced here: 148 us
  Pallas kernels  118 us (79%)
  local copies, waits for them, and re-layouts  26.6 us (18%)
  other arithmetic  4.08 us (3%)
    pallas_call x1, Pallas kernels, shards(): pl.pallas_call(functools.partial(decode_kernel, side, ep, 192.0 ** (-0.5)...  118 us
    unnamed x1, local copies, waits for them, and re-layouts  26.6 us

profile of v1, /device:TPU:1, one launch (start us, length us, event | category | flops | bytes accessed | tf_op | source)
XLA Modules:
  0.0 148.4 jit_solution(1710402932683036821)
XLA Ops:
  0.0 1.4 convert.2.res
  1.4 1.3 reshape.30
  2.7 26.6 %copy.13.cache = bf16[16,1024,576]{2,1,0:T(8,128)(2,1)} copy(bf16[16,1024,576]{1,2,0:T(8,128)(2,1)} %param.12) | data formatting | bytes 37748736 | tf_op args[0]
  29.3 117.7 %decode.1 = f32[8,1,896]{2,1,0:T(1,128)} custom-call(s32[16]{0:T(128)} %lens.1, s32[1,8]{1,0:T(1,128)} %routes.1, f32[1,8]{1,0:T(1,128)} %route_w.1, bf16[16,1024,576]{2,1,0:T(8,128)(2,1)} %copy.13.cache, bf16[16,8,576]{2,1,0:T(8,128)(2,1)} %q.1, bf16[1,512,128]{2,1,0:T(8,128)(2,1)} %upv.1, bf16[1,128,7168]{2,1,0:T(8,128)(2,1)} %outp.1, ...), custom_call_target="tpu_custom_call" | custom-call | tf_op jit(solution)/shard_map/decode/pallas_call | solution.py:407
  147.0 1.4 convert_element_type.16

commit v2 on v1

--- a/solution.py
+++ b/solution.py
@@ -13,7 +13,8 @@
 BF16 = jnp.bfloat16
 masked_score = -1e30
 PAIR = 2
-EXTRA = 128
+LANES = 128
+EXTRA = LANES
 WEIGHT_LANE = 16
 
 
@@ -32,16 +33,16 @@
     side, ep, scale, width,
     lens, routes, route_w, cache, q, upv, outp, res, gain, gate, upw, down,
     out,
-    kbuf, qg, obuf, st_own, st_got, lat, r1, r2_own, r2, latent,
+    kbuf, qg, st1_own, st1, lat, r1, st2_own, st2, r2_own, r2, latent, res32, gain32,
     upg, opr, edr, gu, hv, r5_own, r5, resg, hid, u1, upl, usb, act, r8_own, r8, mix_own, mix_got,
-    k_sem, own_sem, a1_s, a1_r, a2_s, a2_r, st_s, st_r, r1_s, r1_r, r2_s, r2_r,
+    k_sem, own_sem, a1_s, a1_r, a2_s, a2_r, st1_s, st1_r, st2_s, st2_r, r1_s, r1_r, r2_s, r2_r,
     w_s, w_r, x_s, x_r, p_s, p_r, c_s, c_r,
 ):
     seq = side * side
-    batch, span, _ = kbuf.shape
+    batch, _, span = kbuf.shape
     chunks = batch // PAIR
-    heads, lat_dim = obuf.shape[1:]
-    group = heads // seq
+    group, lat_dim = latent.shape[1:]
+    heads = group * seq
     vdim = upv.shape[2]
     cols = opr.shape[2]
     units = gate.shape[2]
@@ -52,7 +53,7 @@
     s_me = lax.axis_index("seq")
     e_me = lax.axis_index("ep")
     x, y = lax.div(s_me, side), lax.rem(s_me, side)
-    core = lax.rem(e_me, 2)
+    z, core = lax.div(e_me, 2), lax.rem(e_me, 2)
     sibling = e_me + 1 - 2 * core
 
     def axes(parity):
@@ -76,9 +77,17 @@
     def other_ep(d):
         return lax.rem(e_me + d, ep)
 
+    left = []
+
+    def finish():
+        for wait in left:
+            wait()
+
     barrier = pltpu.get_barrier_semaphore()
-    each(1, seq, lambda d: pl.semaphore_signal(
-        barrier, inc=1, device_id=(other_seq(d), e_me), device_id_type=MESH))
+    each(1, side, lambda d: pl.semaphore_signal(
+        barrier, inc=1, device_id=(plane(0, lax.rem(x + d, side), y), e_me), device_id_type=MESH))
+    each(1, side, lambda d: pl.semaphore_signal(
+        barrier, inc=1, device_id=(plane(0, x, lax.rem(y + d, side)), e_me), device_id_type=MESH))
     each(1, ep, lambda d: pl.semaphore_signal(
         barrier, inc=1, device_id=(s_me, other_ep(d)), device_id_type=MESH))
 
@@ -90,9 +99,11 @@
     def load_cache(i):
         return pltpu.make_async_copy(cache.at[i], kbuf.at[i], k_sem.at[i])
 
+    slot = core * half + z
+    values_here = pl.ds(pl.multiple_of(z * vdim, vdim), vdim)
     own_weights = [
-        pltpu.make_async_copy(upv.at[0], upg.at[:, pl.ds(pl.multiple_of(e_me * vdim, vdim), vdim)], own_sem.at[chunks]),
-        pltpu.make_async_copy(outp.at[0, :, pl.ds(pl.multiple_of(e_me * cols, cols), cols)], opr.at[e_me], own_sem.at[chunks + 1]),
+        pltpu.make_async_copy(upv.at[0], upg.at[core, :, values_here], own_sem.at[chunks]),
+        pltpu.make_async_copy(outp.at[0, :, pl.ds(pl.multiple_of(e_me * cols, cols), cols)], opr.at[slot], own_sem.at[chunks + 1]),
         pltpu.make_async_copy(down.at[0, :, pl.ds(pl.multiple_of(e_me * cols, cols), cols)], edr.at[e_me], own_sem.at[chunks + 2]),
         pltpu.make_async_copy(gate.at[0], gu.at[:, pl.ds(0, units)], own_sem.at[chunks + 3]),
         pltpu.make_async_copy(upw.at[0], gu.at[:, pl.ds(units, units)], own_sem.at[chunks + 4]),
@@ -101,9 +112,11 @@
     each(0, batch, lambda i: load_cache(i).start())
     for copy in own_weights:
         copy.start()
-    resg[e_me] = res[e_me]
-
-    pl.semaphore_wait(barrier, seq - 1 + ep - 1)
+    res32[...] = res[...].astype(F32)
+    gain32[...] = gain[...].astype(F32)
+    resg[e_me] = res32[e_me]
+
+    pl.semaphore_wait(barrier, 2 * (side - 1) + ep - 1)
 
     def gather_first(c):
         parity = lax.rem(c, 2)
@@ -113,21 +126,39 @@
                  plane(parity, lax.rem(a + d, side), b), e_me)
 
     each(0, chunks, gather_first)
+    left.append(lambda: each(0, chunks, lambda c: drain(qg.at[c, pl.ds(0, side - 1), 0], a1_s.at[c])))
+
+    def spread_values(d):
+        send(upv.at[0], upg.at[core, :, values_here], w_s.at[0], w_r.at[0], s_me, lax.rem(z + d, half) * 2 + core)
+
+    def forward_values():
+        own_weights[0].wait()
+        drain(upg.at[0, :, pl.ds(0, (half - 1) * vdim)], w_r.at[0])
+        send(upg.at[core], upg.at[core], c_s.at[2], c_r.at[2], s_me, sibling)
 
     def spread(d):
         e = other_ep(d)
         here = pl.ds(pl.multiple_of(e * cols, cols), cols)
-        send(upv.at[0], upg.at[:, pl.ds(pl.multiple_of(e_me * vdim, vdim), vdim)], w_s.at[0], w_r.at[0], s_me, e)
-        send(outp.at[0, :, here], opr.at[e_me], w_s.at[1], w_r.at[1], s_me, e)
-        send(res.at[e], resg.at[e_me], w_s.at[3], w_r.at[3], s_me, e)
-
-    def spread_down(d):
-        e = other_ep(d)
+        send(outp.at[0, :, here], opr.at[slot], w_s.at[1], w_r.at[1], s_me, e)
+        send(res32.at[e], resg.at[e_me], w_s.at[3], w_r.at[3], s_me, e)
+
+    def spread_down(hop, flip):
+        e = lax.rem(z + hop, half) * 2 + lax.rem(core + flip, 2)
         here = pl.ds(pl.multiple_of(e * cols, cols), cols)
         send(down.at[0, :, here], edr.at[e_me], w_s.at[2], w_r.at[2], s_me, e)
 
+    far = half // 2
+    each(1, half, spread_values)
     each(1, ep, spread)
-    each(1, ep, spread_down)
+    spread_down(0, 1)
+    for hop in range(1, half):
+        if hop != far:
+            spread_down(hop, 0)
+            spread_down(hop, 1)
+
+    left.append(lambda: drain(upg.at[0, :, pl.ds(0, (half - 1) * vdim)], w_s.at[0]))
+    left.append(lambda: drain(opr.at[pl.ds(0, ep - 1)], w_s.at[1]))
+    left.append(lambda: drain(resg.at[pl.ds(0, ep - 1)], w_s.at[3]))
 
     def gather_second(c):
         parity = lax.rem(c, 2)
@@ -138,13 +169,14 @@
             send(qg.at[c, :, b], qg.at[c, :, b], a2_s.at[c], a2_r.at[c],
                  plane(parity, a, lax.rem(b + d, side)), e_me)
 
-    eye = lax.broadcasted_iota(jnp.int32, (heads, heads), 0) == lax.broadcasted_iota(jnp.int32, (heads, heads), 1)
-
-    def to_row(column):
-        return jnp.sum(jnp.where(eye, column, 0.0), axis=0, keepdims=True)
-
-    def to_column(row):
-        return jnp.sum(jnp.where(eye, row, 0.0), axis=1, keepdims=True)
+    def diagonal(rows, first):
+        lane = lax.broadcasted_iota(jnp.int32, (rows, heads), 1)
+        return lane == first + lax.broadcasted_iota(jnp.int32, (rows, heads), 0)
+
+    eye = diagonal(heads, 0)
+
+    def to_column(row, mask):
+        return jnp.sum(jnp.where(mask, row, 0.0), axis=1, keepdims=True)
 
     position = s_me * span + lax.broadcasted_iota(jnp.int32, (1, span), 1)
 
@@ -154,79 +186,97 @@
             i = c * PAIR + j
             load_cache(i).wait()
             queries = qg[c, :, :, j].astype(F32).reshape(heads, -1).astype(BF16)
-            scores = lax.dot_general(queries, kbuf[i], (((1,), (1,)), ((), ())), preferred_element_type=F32)
+            scores = jnp.dot(queries, kbuf[i], preferred_element_type=F32)
             live = position < lens[i]
             scores = jnp.where(live, scores, masked_score)
             top = jnp.max(scores, axis=1, keepdims=True)
             prob = jnp.where(live, jnp.exp2((scores - top) * (scale * math.log2(math.e))), 0.0)
             total = jnp.sum(prob, axis=1, keepdims=True)
-            obuf[i] = jnp.dot(prob.astype(BF16), kbuf[i, :, :lat_dim], preferred_element_type=F32)
-            st_own[c, j:j + 1] = to_row(top)
-            st_own[c, PAIR + j:PAIR + j + 1] = to_row(total)
-        each(1, seq, lambda d: send(
-            st_own.at[c], st_got.at[c, d - 1], st_s.at[c], st_r.at[c], other_seq(d), e_me))
-
-    def scale_own(c):
+            total = jnp.maximum(total, 1.0)
+            mean = lax.dot_general(
+                prob.astype(BF16), kbuf[i, :lat_dim], (((1,), (1,)), ((), ())), preferred_element_type=F32) / total
+            lat[c, :, j] = mean.reshape(side, side * group, lat_dim).astype(BF16)
+            level = top * scale + jnp.log(total)
+            st1_own[c, j:j + 1] = jnp.sum(jnp.where(eye, level, 0.0), axis=0, keepdims=True)
         parity = lax.rem(c, 2)
         a, b = axes(parity)
-        drain(st_got.at[c], st_r.at[c])
-        own = st_own[c]
-        got = st_got[c]
-        own_top, own_total = own[:PAIR], own[PAIR:]
-        tops, totals = got[:, :PAIR], got[:, PAIR:]
-        top = jnp.maximum(own_top, jnp.max(tops, axis=0))
-        own_factor = jnp.exp((own_top - top) * scale)
-        den = own_total * own_factor + jnp.sum(totals * jnp.exp((tops - top[None]) * scale), axis=0)
-        factor = own_factor / den
-        for j in range(PAIR):
-            scaled = obuf[c * PAIR + j] * to_column(factor[j:j + 1])
-            lat[c, :, j] = scaled.reshape(side, side * group, lat_dim).astype(BF16)
         for d in range(1, side):
             to = lax.rem(a + d, side)
+            send(st1_own.at[c], st1.at[c, d - 1], st1_s.at[c], st1_r.at[c], plane(parity, to, b), e_me)
             send(lat.at[c, to], r1.at[c, d - 1], r1_s.at[c], r1_r.at[c], plane(parity, to, b), e_me)
+
+    def merge(own_level, levels):
+        top = jnp.maximum(own_level, jnp.max(levels, axis=0))
+        weights = [jnp.exp(own_level - top)] + [jnp.exp(levels[d] - top) for d in range(side - 1)]
+        den = sum(weights)
+        return top + jnp.log(den), [w / den for w in weights]
 
     def sum_first(c):
         parity = lax.rem(c, 2)
         a, b = axes(parity)
+        drain(st1.at[c], st1_r.at[c])
+        level, weights = merge(st1_own[c], st1[c])
+        st2_own[c] = level
+        mask = diagonal(side * group, a * side * group)
         drain(r1.at[c], r1_r.at[c])
         for j in range(PAIR):
-            total = lat[c, a, j].astype(F32)
+            total = lat[c, a, j].astype(F32) * to_column(weights[0][j:j + 1], mask)
             for d in range(side - 1):
-                total += r1[c, d, j].astype(F32)
+                total += r1[c, d, j].astype(F32) * to_column(weights[d + 1][j:j + 1], mask)
             r2_own[c, :, j] = total.reshape(side, group, lat_dim).astype(BF16)
         for d in range(1, side):
             to = lax.rem(b + d, side)
+            send(st2_own.at[c], st2.at[c, d - 1], st2_s.at[c], st2_r.at[c], plane(parity, a, to), e_me)
             send(r2_own.at[c, to], r2.at[c, d - 1], r2_s.at[c], r2_r.at[c], plane(parity, a, to), e_me)
 
     def sum_second(c):
         a, b = axes(lax.rem(c, 2))
+        drain(st2.at[c], st2_r.at[c])
+        _, weights = merge(st2_own[c], st2[c])
+        mask = diagonal(group, (a * side + b) * group)
         drain(r2.at[c], r2_r.at[c])
-        total = r2_own[c, b].astype(F32)
-        for d in range(side - 1):
-            total += r2[c, d].astype(F32)
-        latent[pl.ds(c * PAIR, PAIR)] = total
-
-    ahead = 2
-    each(0, min(ahead, chunks), gather_second)
+        for j in range(PAIR):
+            total = r2_own[c, b, j].astype(F32) * to_column(weights[0][j:j + 1], mask)
+            for d in range(side - 1):
+                total += r2[c, d, j].astype(F32) * to_column(weights[d + 1][j:j + 1], mask)
+            latent[c * PAIR + j] = total
+
+    each(0, chunks, gather_second)
+    lag = 3
 
     def stage(i):
-        pl.when(i < chunks)(lambda: attend(i))
-        pl.when(i + ahead < chunks)(lambda: gather_second(i + ahead))
-        pl.when(jnp.logical_and(i >= 1, i < chunks + 1))(lambda: scale_own(i - 1))
-        pl.when(jnp.logical_and(i >= 2, i < chunks + 2))(lambda: sum_first(i - 2))
-        pl.when(i >= 3)(lambda: sum_second(i - 3))
-
-    each(0, chunks + 3, stage)
-
-    own_weights[0].wait()
-    drain(upg.at[:, pl.ds(0, (ep - 1) * vdim)], w_r.at[0])
+        pl.when(i == chunks // 2)(forward_values)
+
+        def at(step, low):
+            c = i - low * lag
+            pl.when(jnp.logical_and(c >= 0, c < chunks))(lambda: step(c))
+
+        at(attend, 0)
+        at(sum_first, 1)
+        at(sum_second, 2)
+
+    each(0, chunks + 2 * lag, stage)
+
+    def sent(c):
+        drain(qg.at[c, pl.ds(0, side - 1)], a2_s.at[c])
+        drain(st1.at[c], st1_s.at[c])
+        drain(st2.at[c], st2_s.at[c])
+        drain(r1.at[c], r1_s.at[c])
+        drain(r2.at[c], r2_s.at[c])
+
+    left.append(lambda: each(0, chunks, sent))
+    left.append(lambda: drain(upg.at[0], c_s.at[2]))
+
+    drain(upg.at[0], c_r.at[2])
     latents = latent[...].reshape(batch * group, lat_dim).astype(BF16)
-    values = jnp.dot(latents, upg[...], preferred_element_type=F32)
+    values = jnp.concatenate(
+        [jnp.dot(latents, upg[k], preferred_element_type=F32) for k in range(2)], axis=1)
     row = lax.broadcasted_iota(jnp.int32, values.shape, 0)
-    column = lax.broadcasted_iota(jnp.int32, values.shape, 1)
-    values = jnp.where(lax.rem(row, group) == lax.div(column, vdim), values, 0.0)
+    block = lax.div(lax.broadcasted_iota(jnp.int32, values.shape, 1), vdim)
+    values = jnp.where(lax.rem(row, group) == lax.rem(block, half) * 2 + lax.div(block, half), values, 0.0)
     hv[e_me] = jnp.sum(values.reshape(batch, group, group * vdim), axis=1).astype(BF16)
     each(1, ep, lambda d: send(hv.at[e_me], hv.at[e_me], x_s.at[0], x_r.at[0], s_me, other_ep(d)))
+    left.append(lambda: drain(hv.at[pl.ds(0, ep - 1)], x_s.at[0]))
 
     own_weights[1].wait()
     drain(opr.at[pl.ds(0, ep - 1)], w_r.at[1])
@@ -236,6 +286,7 @@
     r5_own[...] = attended.reshape(seq, ep, cols).astype(BF16)
     each(1, seq, lambda d: send(
         r5_own.at[other_seq(d)], r5.at[d - 1], x_s.at[1], x_r.at[1], other_seq(d), e_me))
+    left.append(lambda: drain(r5, x_s.at[1]))
 
     drain(resg.at[pl.ds(0, ep - 1)], w_r.at[3])
     residual = resg[...].reshape(ep, cols)
@@ -258,11 +309,17 @@
     hid[...] = hidden
     s_high, s_mid, s_low = three_parts(jnp.sum(hidden * hidden, axis=1, keepdims=True))
     squares = jnp.where(lane == 0, s_high, jnp.where(lane == 1, s_mid, jnp.where(lane == 2, s_low, 0.0)))
-    u1[e_me, :, :cols] = (hidden * gain[e_me]).astype(BF16)
+    per = cols // LANES
+    gain_row = jnp.concatenate([gain32[pl.ds(e_me * per + k, 1), :] for k in range(per)], axis=1)
+    u1[e_me, :, :cols] = (hidden * gain_row).astype(BF16)
     u1[e_me, :, cols:] = (squares + weight).astype(BF16)
     each(1, ep, lambda d: send(u1.at[e_me], u1.at[e_me], x_s.at[2], x_r.at[2], s_me, other_ep(d)))
+    left.append(lambda: drain(u1.at[pl.ds(0, ep - 1)], x_s.at[2]))
 
     drain(u1.at[pl.ds(0, ep - 1)], x_r.at[2])
+    spread_down(far, 0)
+    spread_down(far, 1)
+    left.append(lambda: drain(edr.at[pl.ds(0, ep - 1)], w_s.at[2]))
     for t in range(2):
         a, b = axes(t)
         upl[t, a, b] = u1[pl.ds(core * half + t * quarter, quarter)]
@@ -276,6 +333,14 @@
     for t in range(2):
         drain(upl.at[t, pl.ds(0, side - 1)], p_r.at[2 + t])
         send(upl.at[t], usb.at[t], c_s.at[t], c_r.at[t], s_me, sibling)
+
+    def sent_rows():
+        for t in range(2):
+            drain(upl.at[t, pl.ds(0, side - 1), 0], p_s.at[t])
+            drain(upl.at[t, pl.ds(0, side - 1)], p_s.at[2 + t])
+            drain(usb.at[t], c_s.at[t])
+
+    left.append(sent_rows)
 
     own_weights[3].wait()
     own_weights[4].wait()
@@ -306,6 +371,7 @@
     gate_pre, up_pre = gated[:, :units], gated[:, units:]
     act[e_me] = (gate_pre / (1.0 + jnp.exp(-gate_pre)) * up_pre).astype(BF16)
     each(1, ep, lambda d: send(act.at[e_me], act.at[e_me], x_s.at[3], x_r.at[3], s_me, other_ep(d)))
+    left.append(lambda: drain(act.at[pl.ds(0, ep - 1)], x_s.at[3]))
 
     own_weights[2].wait()
     drain(edr.at[pl.ds(0, ep - 1)], w_r.at[2])
@@ -315,6 +381,7 @@
     r8_own[...] = result.reshape(seq, ep, cols).astype(BF16)
     each(1, seq, lambda d: send(
         r8_own.at[other_seq(d)], r8.at[d - 1], x_s.at[4], x_r.at[4], other_seq(d), e_me))
+    left.append(lambda: drain(r8, x_s.at[4]))
 
     drain(r8, x_r.at[4])
     mixed = r8_own[s_me].astype(F32)
@@ -325,31 +392,11 @@
     mix_got[e_me] = mix_own[e_me]
     each(1, ep, lambda d: send(
         mix_own.at[other_ep(d)], mix_got.at[e_me], x_s.at[5], x_r.at[5], s_me, other_ep(d)))
+    left.append(lambda: drain(mix_got.at[pl.ds(0, ep - 1)], x_s.at[5]))
     drain(mix_got.at[pl.ds(0, ep - 1)], x_r.at[5])
     out[...] = mix_got[...]
 
-    def sent(c):
-        drain(qg.at[c, pl.ds(0, side - 1), 0], a1_s.at[c])
-        drain(qg.at[c, pl.ds(0, side - 1)], a2_s.at[c])
-        drain(st_got.at[c], st_s.at[c])
-        drain(r1.at[c], r1_s.at[c])
-        drain(r2.at[c], r2_s.at[c])
-
-    each(0, chunks, sent)
-    drain(upg.at[:, pl.ds(0, (ep - 1) * vdim)], w_s.at[0])
-    drain(opr.at[pl.ds(0, ep - 1)], w_s.at[1])
-    drain(edr.at[pl.ds(0, ep - 1)], w_s.at[2])
-    drain(resg.at[pl.ds(0, ep - 1)], w_s.at[3])
-    drain(hv.at[pl.ds(0, ep - 1)], x_s.at[0])
-    drain(r5, x_s.at[1])
-    drain(u1.at[pl.ds(0, ep - 1)], x_s.at[2])
-    drain(act.at[pl.ds(0, ep - 1)], x_s.at[3])
-    drain(r8, x_s.at[4])
-    drain(mix_got.at[pl.ds(0, ep - 1)], x_s.at[5])
-    for t in range(2):
-        drain(upl.at[t, pl.ds(0, side - 1), 0], p_s.at[t])
-        drain(upl.at[t, pl.ds(0, side - 1)], p_s.at[2 + t])
-        drain(usb.at[t], c_s.at[t])
+    finish()
 
 
 def shards(
@@ -369,17 +416,20 @@
     dma = pltpu.SemaphoreType.DMA
     vmem = pltpu.VMEM
     scratch = [
-        vmem((batch, span, kdim), BF16),
+        vmem((batch, kdim, span), BF16),
         vmem((chunks, side, side, PAIR, group, kdim), BF16),
-        vmem((batch, heads, lat_dim), F32),
-        vmem((chunks, 2 * PAIR, heads), F32),
-        vmem((chunks, seq - 1, 2 * PAIR, heads), F32),
+        vmem((chunks, PAIR, heads), F32),
+        vmem((chunks, side - 1, PAIR, heads), F32),
         vmem((chunks, side, PAIR, side * group, lat_dim), BF16),
         vmem((chunks, side - 1, PAIR, side * group, lat_dim), BF16),
+        vmem((chunks, PAIR, heads), F32),
+        vmem((chunks, side - 1, PAIR, heads), F32),
         vmem((chunks, side, PAIR, group, lat_dim), BF16),
         vmem((chunks, side - 1, PAIR, group, lat_dim), BF16),
         vmem((batch, group, lat_dim), F32),
-        vmem((lat_dim, ep * vdim), BF16),
+        vmem((ep, 1, cols), F32),
+        vmem((width // LANES, LANES), F32),
+        vmem((2, lat_dim, ep // 2 * vdim), BF16),
         vmem((ep, vdim, cols), BF16),
         vmem((ep, units, cols), BF16),
         vmem((width, 2 * units), BF16),
@@ -399,8 +449,8 @@
         dma((batch,)),
         dma((chunks + 5,)),
     ]
-    scratch += [dma((chunks,)) for _ in range(10)]
-    scratch += [dma((4,)), dma((4,)), dma((6,)), dma((6,)), dma((4,)), dma((4,)), dma((2,)), dma((2,))]
+    scratch += [dma((chunks,)) for _ in range(12)]
+    scratch += [dma((4,)), dma((4,)), dma((6,)), dma((6,)), dma((4,)), dma((4,)), dma((3,)), dma((3,))]
     smem = pl.BlockSpec(memory_space=pltpu.SMEM)
     whole = pl.BlockSpec(memory_space=pltpu.VMEM)
     anywhere = pl.BlockSpec(memory_space=pl.ANY)
@@ -414,8 +464,8 @@
             collective_id=0, has_side_effects=True, vmem_limit_bytes=58 * 1024 * 1024),
         name="decode",
     )(
-        lengths, routes, route_weight, latent_cache, queries, up_value, out_proj,
-        residual.astype(F32).reshape(ep, 1, cols), norm_gain.astype(F32).reshape(ep, 1, cols),
+        lengths, routes, route_weight, jnp.swapaxes(latent_cache, 1, 2), queries, up_value, out_proj,
+        residual.reshape(ep, 1, cols), norm_gain.reshape(width // LANES, LANES),
         expert_gate, expert_up, expert_down,
     )
     return mixed.reshape(1, width).astype(BF16)

time: 149 us -> 98.9 us (0.66)
  local copies, waits for them, and re-layouts: 26.6 us -> 0 us
  Pallas kernels: 118 us -> 97.3 us
  other arithmetic: 4.08 us -> 1.38 us
    unnamed x1 -> x0, local copies, waits for them, and re-layouts: 26.6 us -> none
    pallas_call x1, Pallas kernels: 118 us -> 97.3 us  [shards(): pl.pallas_call(functools.partial(decode_kernel, side, ep, 192.0 ** (-0.5)...]
    reshape x2 -> x0, other arithmetic: 2.7 us -> none  [the longest x1 1.39 us: shards(): residual.astype(F32).reshape(ep, 1, cols)]
where the time goes in v2:
time: 98.9 us; the launch traced here: 98.6 us
  Pallas kernels  97.3 us (98%)
  other arithmetic  1.38 us (1%)
    pallas_call x1, Pallas kernels, shards(): pl.pallas_call(functools.partial(decode_kernel, side, ep, 192.0 ** (-0.5)...  97.3 us

profile of v2, /device:TPU:1, one launch (start us, length us, event | category | flops | bytes accessed | tf_op | source)
XLA Modules:
  0.0 98.6 jit_solution(10511868770962037412)
XLA Ops:
  0.0 97.3 %decode.1 = f32[8,1,896]{2,1,0:T(1,128)} custom-call(s32[16]{0:T(128)} %lens.1, s32[1,8]{1,0:T(1,128)} %routes.1, f32[1,8]{1,0:T(1,128)} %route_w.1, bf16[16,576,1024]{2,1,0:T(8,128)(2,1)} %bitcast.4, bf16[16,8,576]{2,1,0:T(8,128)(2,1)} %q.1, bf16[1,512,128]{2,1,0:T(8,128)(2,1)} %upv.1, bf16[1,128,7168]{2,1,0:T(8,128)(2,1)} %outp.1, ...), custom_call_target="tpu_custom_call" | custom-call | tf_op jit(solution)/shard_map/decode/pallas_call | solution.py:457
  97.3 1.4 %convert_element_type.14 = bf16[8,1,896]{2,1,0:T(2,128)(2,1)} convert(f32[8,1,896]{2,1,0:T(1,128)} %decode.1) | non-fusion elementwise | flops 7168 | bytes 43008 | tf_op jit(solution)/shard_map/convert_element_type | solution.py:471

commit v3 on v2

--- a/solution.py
+++ b/solution.py
@@ -25,6 +25,11 @@
     return high, middle, (rest - middle).astype(BF16).astype(F32)
 
 
+def row_cuts(cols):
+    tiles = (cols + EXTRA) // LANES
+    return [LANES * (tiles * p // 3) for p in range(3)] + [cols + EXTRA]
+
+
 def drain(ref, sem):
     pltpu.make_async_copy(ref, ref, sem).wait()
 
@@ -33,10 +38,10 @@
     side, ep, scale, width,
     lens, routes, route_w, cache, q, upv, outp, res, gain, gate, upw, down,
     out,
-    kbuf, qg, st1_own, st1, lat, r1, st2_own, st2, r2_own, r2, latent, res32, gain32,
-    upg, opr, edr, gu, hv, r5_own, r5, resg, hid, u1, upl, usb, act, r8_own, r8, mix_own, mix_got,
-    k_sem, own_sem, a1_s, a1_r, a2_s, a2_r, st1_s, st1_r, st2_s, st2_r, r1_s, r1_r, r2_s, r2_r,
-    w_s, w_r, x_s, x_r, p_s, p_r, c_s, c_r,
+    kbuf, qraw, qg, st1_own, st1, lat, r1, st2_own, st2, r2_own, r2, latent, res32, gain32,
+    upg, opr, edr, gu, hv, r5_own, r5, resg, hid, rows_a, rows_b, rows_c, rows_oa, rows_ob, rows_oc, act, r8_own, r8, mix_own, mix_got,
+    k_sem, own_sem, a1_s, a1_r, a2_s, a2_r, a3_s, a3_r, st1_s, st1_r, st2_s, st2_r, r1_s, r1_r, r2_s, r2_r,
+    w_s, w_r, x_s, x_r, p_s, p_r, c_s, c_r, h_s, h_r,
 ):
     seq = side * side
     batch, _, span = kbuf.shape
@@ -47,7 +52,6 @@
     cols = opr.shape[2]
     units = gate.shape[2]
     half = ep // 2
-    quarter = ep // 4
     rows_all = seq * ep
 
     s_me = lax.axis_index("seq")
@@ -77,6 +81,8 @@
     def other_ep(d):
         return lax.rem(e_me + d, ep)
 
+    cuts = row_cuts(cols)
+    rows_p, rows_o = (rows_a, rows_b, rows_c), (rows_oa, rows_ob, rows_oc)
     left = []
 
     def finish():
@@ -91,10 +97,8 @@
     each(1, ep, lambda d: pl.semaphore_signal(
         barrier, inc=1, device_id=(s_me, other_ep(d)), device_id_type=MESH))
 
-    def own_query(c):
-        a, b = axes(lax.rem(c, 2))
-        return pltpu.make_async_copy(
-            q.at[pl.ds(c * PAIR, PAIR)], qg.at[c, a, b], own_sem.at[c])
+    load_queries = pltpu.make_async_copy(q, qraw, own_sem.at[chunks + 5])
+    load_queries.start()
 
     def load_cache(i):
         return pltpu.make_async_copy(cache.at[i], kbuf.at[i], k_sem.at[i])
@@ -108,7 +112,6 @@
         pltpu.make_async_copy(gate.at[0], gu.at[:, pl.ds(0, units)], own_sem.at[chunks + 3]),
         pltpu.make_async_copy(upw.at[0], gu.at[:, pl.ds(units, units)], own_sem.at[chunks + 4]),
     ]
-    each(0, chunks, lambda c: own_query(c).start())
     each(0, batch, lambda i: load_cache(i).start())
     for copy in own_weights:
         copy.start()
@@ -116,13 +119,22 @@
     gain32[...] = gain[...].astype(F32)
     resg[e_me] = res32[e_me]
 
+
+    def pack(c):
+        a, b = axes(lax.rem(c, 2))
+        rows = [qraw[c * PAIR + j].astype(F32) for j in range(PAIR)]
+        row = jnp.concatenate([r[:, :lat_dim] for r in rows] + [r[:, lat_dim:] for r in rows], axis=1)
+        qg[c, a, b] = row.astype(BF16)
+
+    load_queries.wait()
+    each(0, chunks, pack)
     pl.semaphore_wait(barrier, 2 * (side - 1) + ep - 1)
 
     def gather_first(c):
         parity = lax.rem(c, 2)
         a, b = axes(parity)
         for d in range(1, side):
-            send(q.at[pl.ds(c * PAIR, PAIR)], qg.at[c, a, b], a1_s.at[c], a1_r.at[c],
+            send(qg.at[c, a, b], qg.at[c, a, b], a1_s.at[c], a1_r.at[c],
                  plane(parity, lax.rem(a + d, side), b), e_me)
 
     each(0, chunks, gather_first)
@@ -163,11 +175,19 @@
     def gather_second(c):
         parity = lax.rem(c, 2)
         a, b = axes(parity)
-        own_query(c).wait()
         drain(qg.at[c, pl.ds(0, side - 1), 0], a1_r.at[c])
-        for d in range(1, side):
+        for d in (1, side - 1):
             send(qg.at[c, :, b], qg.at[c, :, b], a2_s.at[c], a2_r.at[c],
                  plane(parity, a, lax.rem(b + d, side)), e_me)
+
+    def gather_third(c):
+        parity = lax.rem(c, 2)
+        a, b = axes(parity)
+        drain(qg.at[c, pl.ds(0, 2)], a2_r.at[c])
+        for d, first in ((1, 0), (side - 1, side // 2)):
+            to, came = lax.rem(b + d, side), lax.rem(b + side - d, side)
+            part = qg.at[c, pl.ds(first, side // 2), came]
+            send(part, part, a3_s.at[c], a3_r.at[c], plane(parity, a, to), e_me)
 
     def diagonal(rows, first):
         lane = lax.broadcasted_iota(jnp.int32, (rows, heads), 1)
@@ -181,20 +201,24 @@
     position = s_me * span + lax.broadcasted_iota(jnp.int32, (1, span), 1)
 
     def attend(c):
-        drain(qg.at[c, pl.ds(0, side - 1)], a2_r.at[c])
+        drain(qg.at[c, 0], a3_r.at[c])
         for j in range(PAIR):
-            i = c * PAIR + j
-            load_cache(i).wait()
-            queries = qg[c, :, :, j].astype(F32).reshape(heads, -1).astype(BF16)
-            scores = jnp.dot(queries, kbuf[i], preferred_element_type=F32)
-            live = position < lens[i]
-            scores = jnp.where(live, scores, masked_score)
-            top = jnp.max(scores, axis=1, keepdims=True)
-            prob = jnp.where(live, jnp.exp2((scores - top) * (scale * math.log2(math.e))), 0.0)
+            load_cache(c * PAIR + j).wait()
+        packed = qg[c].astype(F32).reshape(heads, -1)
+        split = PAIR * lat_dim
+        rotary = (packed.shape[1] - split) // PAIR
+        scores = [jnp.dot(
+            jnp.concatenate([packed[:, j * lat_dim:(j + 1) * lat_dim],
+                             packed[:, split + j * rotary:split + (j + 1) * rotary]], axis=1).astype(BF16),
+            kbuf[c * PAIR + j], preferred_element_type=F32) for j in range(PAIR)]
+        for j in range(PAIR):
+            masked = jnp.where(position < lens[c * PAIR + j], scores[j], masked_score)
+            top = jnp.max(masked, axis=1, keepdims=True)
+            prob = jnp.exp2((masked - top) * (scale * math.log2(math.e)))
             total = jnp.sum(prob, axis=1, keepdims=True)
-            total = jnp.maximum(total, 1.0)
             mean = lax.dot_general(
-                prob.astype(BF16), kbuf[i, :lat_dim], (((1,), (1,)), ((), ())), preferred_element_type=F32) / total
+                prob.astype(BF16), kbuf[c * PAIR + j, :lat_dim], (((1,), (1,)), ((), ())),
+                preferred_element_type=F32) / total
             lat[c, :, j] = mean.reshape(side, side * group, lat_dim).astype(BF16)
             level = top * scale + jnp.log(total)
             st1_own[c, j:j + 1] = jnp.sum(jnp.where(eye, level, 0.0), axis=0, keepdims=True)
@@ -241,24 +265,45 @@
                 total += r2[c, d, j].astype(F32) * to_column(weights[d + 1][j:j + 1], mask)
             latent[c * PAIR + j] = total
 
-    each(0, chunks, gather_second)
-    lag = 3
+    window = 4
+    each(0, min(window, chunks), gather_second)
+    ahead = 2
+    lag = 2
+
+    def share_values(part):
+        rows = batch // 2
+        latents = latent[pl.ds(part * rows, rows)].reshape(rows * group, lat_dim).astype(BF16)
+        values = jnp.concatenate([jnp.dot(latents, upg[k], preferred_element_type=F32) for k in range(2)], axis=1)
+        row = lax.broadcasted_iota(jnp.int32, values.shape, 0)
+        block = lax.div(lax.broadcasted_iota(jnp.int32, values.shape, 1), vdim)
+        values = jnp.where(lax.rem(row, group) == lax.rem(block, half) * 2 + lax.div(block, half), values, 0.0)
+        hv[e_me, part] = jnp.sum(values.reshape(rows, group, group * vdim), axis=1).astype(BF16)
+        each(1, ep, lambda d: send(
+            hv.at[e_me, part], hv.at[e_me, part], h_s.at[part], h_r.at[part], s_me, other_ep(d)))
+
+    def first_values():
+        drain(upg.at[0], c_r.at[2])
+        share_values(0)
 
     def stage(i):
         pl.when(i == chunks // 2)(forward_values)
 
-        def at(step, low):
-            c = i - low * lag
+        def at(step, after):
+            c = i - after
             pl.when(jnp.logical_and(c >= 0, c < chunks))(lambda: step(c))
 
-        at(attend, 0)
-        at(sum_first, 1)
-        at(sum_second, 2)
-
-    each(0, chunks + 2 * lag, stage)
+        at(gather_third, 0)
+        at(gather_second, -window)
+        at(attend, ahead)
+        at(sum_first, ahead + lag)
+        at(sum_second, ahead + 2 * lag)
+        pl.when(i == chunks // 2 - 1 + ahead + 2 * lag)(first_values)
+
+    each(0, chunks + ahead + 2 * lag, stage)
 
     def sent(c):
-        drain(qg.at[c, pl.ds(0, side - 1)], a2_s.at[c])
+        drain(qg.at[c, pl.ds(0, 2)], a2_s.at[c])
+        drain(qg.at[c, 0], a3_s.at[c])
         drain(st1.at[c], st1_s.at[c])
         drain(st2.at[c], st2_s.at[c])
         drain(r1.at[c], r1_s.at[c])
@@ -267,22 +312,14 @@
     left.append(lambda: each(0, chunks, sent))
     left.append(lambda: drain(upg.at[0], c_s.at[2]))
 
-    drain(upg.at[0], c_r.at[2])
-    latents = latent[...].reshape(batch * group, lat_dim).astype(BF16)
-    values = jnp.concatenate(
-        [jnp.dot(latents, upg[k], preferred_element_type=F32) for k in range(2)], axis=1)
-    row = lax.broadcasted_iota(jnp.int32, values.shape, 0)
-    block = lax.div(lax.broadcasted_iota(jnp.int32, values.shape, 1), vdim)
-    values = jnp.where(lax.rem(row, group) == lax.rem(block, half) * 2 + lax.div(block, half), values, 0.0)
-    hv[e_me] = jnp.sum(values.reshape(batch, group, group * vdim), axis=1).astype(BF16)
-    each(1, ep, lambda d: send(hv.at[e_me], hv.at[e_me], x_s.at[0], x_r.at[0], s_me, other_ep(d)))
-    left.append(lambda: drain(hv.at[pl.ds(0, ep - 1)], x_s.at[0]))
-
+    share_values(1)
     own_weights[1].wait()
     drain(opr.at[pl.ds(0, ep - 1)], w_r.at[1])
-    drain(hv.at[pl.ds(0, ep - 1)], x_r.at[0])
+    for part in range(2):
+        drain(hv.at[pl.ds(0, ep - 1), part], h_r.at[part])
+        left.append(lambda part=part: drain(hv.at[pl.ds(0, ep - 1), part], h_s.at[part]))
     attended = jnp.dot(
-        hv[...].reshape(rows_all, group * vdim), opr[...].reshape(ep * vdim, cols), preferred_element_type=F32)
+        hv[...].astype(F32).reshape(rows_all, group * vdim).astype(BF16), opr[...].reshape(ep * vdim, cols), preferred_element_type=F32)
     r5_own[...] = attended.reshape(seq, ep, cols).astype(BF16)
     each(1, seq, lambda d: send(
         r5_own.at[other_seq(d)], r5.at[d - 1], x_s.at[1], x_r.at[1], other_seq(d), e_me))
@@ -311,34 +348,45 @@
     squares = jnp.where(lane == 0, s_high, jnp.where(lane == 1, s_mid, jnp.where(lane == 2, s_low, 0.0)))
     per = cols // LANES
     gain_row = jnp.concatenate([gain32[pl.ds(e_me * per + k, 1), :] for k in range(per)], axis=1)
-    u1[e_me, :, :cols] = (hidden * gain_row).astype(BF16)
-    u1[e_me, :, cols:] = (squares + weight).astype(BF16)
-    each(1, ep, lambda d: send(u1.at[e_me], u1.at[e_me], x_s.at[2], x_r.at[2], s_me, other_ep(d)))
-    left.append(lambda: drain(u1.at[pl.ds(0, ep - 1)], x_s.at[2]))
-
-    drain(u1.at[pl.ds(0, ep - 1)], x_r.at[2])
+    row = jnp.concatenate([hidden * gain_row, squares + weight], axis=1).astype(BF16)
+
+    def place(p, first, second, third):
+        px, py, pz = ((first, second, third), (third, first, second), (second, third, first))[p]
+        return px * side + py, pz * 2 + core
+
+    here = ((x, y, z), (y, z, x), (z, x, y))
+    for p in range(3):
+        first, second, third = here[p]
+        mine = first * side + second
+        rows_p[p][third, mine] = row[:, cuts[p]:cuts[p + 1]]
+
+        def to_plane(i, p=p, first=first, second=second, third=third, mine=mine):
+            s, e = place(p, lax.rem(first + lax.div(i, side), side), lax.rem(second + lax.rem(i, side), side), third)
+            send(rows_p[p].at[third, mine], rows_p[p].at[third, mine], p_s.at[p], p_r.at[p], s, e)
+
+        each(1, seq, to_plane)
+    for p in range(3):
+        first, second, third = here[p]
+        drain(rows_p[p].at[0, pl.ds(0, seq - 1)], p_r.at[p])
+        for d in range(1, side):
+            s, e = place(p, first, second, lax.rem(third + d, side))
+            send(rows_p[p].at[third], rows_p[p].at[third], p_s.at[3 + p], p_r.at[3 + p], s, e)
+        send(rows_p[p].at[third], rows_o[p].at[third], c_s.at[3 + p], c_r.at[3 + p], s_me, sibling)
     spread_down(far, 0)
     spread_down(far, 1)
     left.append(lambda: drain(edr.at[pl.ds(0, ep - 1)], w_s.at[2]))
-    for t in range(2):
-        a, b = axes(t)
-        upl[t, a, b] = u1[pl.ds(core * half + t * quarter, quarter)]
+    for p in range(3):
+        third = here[p][2]
+        drain(rows_p[p].at[pl.ds(0, side - 1)], p_r.at[3 + p])
         for d in range(1, side):
-            send(upl.at[t, a, b], upl.at[t, a, b], p_s.at[t], p_r.at[t], plane(t, lax.rem(a + d, side), b), e_me)
-    for t in range(2):
-        a, b = axes(t)
-        drain(upl.at[t, pl.ds(0, side - 1), 0], p_r.at[t])
-        for d in range(1, side):
-            send(upl.at[t, :, b], upl.at[t, :, b], p_s.at[2 + t], p_r.at[2 + t], plane(t, a, lax.rem(b + d, side)), e_me)
-    for t in range(2):
-        drain(upl.at[t, pl.ds(0, side - 1)], p_r.at[2 + t])
-        send(upl.at[t], usb.at[t], c_s.at[t], c_r.at[t], s_me, sibling)
+            at_d = lax.rem(third + d, side)
+            send(rows_p[p].at[at_d], rows_o[p].at[at_d], c_s.at[3 + p], c_r.at[3 + p], s_me, sibling)
 
     def sent_rows():
-        for t in range(2):
-            drain(upl.at[t, pl.ds(0, side - 1), 0], p_s.at[t])
-            drain(upl.at[t, pl.ds(0, side - 1)], p_s.at[2 + t])
-            drain(usb.at[t], c_s.at[t])
+        for p in range(3):
+            drain(rows_p[p].at[0, pl.ds(0, seq - 1)], p_s.at[p])
+            drain(rows_p[p].at[pl.ds(0, side - 1)], p_s.at[3 + p])
+            drain(rows_o[p], c_s.at[3 + p])
 
     left.append(sent_rows)
 
@@ -346,21 +394,22 @@
     own_weights[4].wait()
     gated = jnp.zeros((rows_all, 2 * units), F32)
     extra = jnp.zeros((rows_all, EXTRA), F32)
-    for which in range(2):
-        for t in range(2):
-            buf = (upl, usb)[which]
-            if which:
-                drain(usb.at[t], c_r.at[t])
-            first = (core + which * (1 - 2 * core)) * half + t * quarter
-            for k in range(quarter):
-                rows = [
-                    (buf[t, i, j, k] if t == 0 else buf[t, j, i, k]).astype(F32)
-                    for i in range(side) for j in range(side)
-                ]
-                rows = jnp.concatenate(rows, axis=0)
-                at = pl.ds(pl.multiple_of((first + k) * cols, cols), cols)
-                gated += jnp.dot(rows[:, :cols].astype(BF16), gu[at, :], preferred_element_type=F32)
-                extra += rows[:, cols:]
+    for other in range(2):
+        if other:
+            for p in range(3):
+                drain(rows_o[p], c_r.at[3 + p])
+        bufs = (rows_p, rows_o)[other]
+        for k in range(side):
+            parts = []
+            for p in range(3):
+                at_p = [((k, i * side + j), (i, j * side + k), (j, k * side + i))[p]
+                        for i in range(side) for j in range(side)]
+                parts.append(jnp.concatenate([bufs[p][at].astype(F32) for at in at_p], axis=0))
+            rows = jnp.concatenate(parts, axis=1)
+            e = 2 * k + core + other * (1 - 2 * core)
+            span_e = pl.ds(pl.multiple_of(e * cols, cols), cols)
+            gated += jnp.dot(rows[:, :cols].astype(BF16), gu[span_e, :], preferred_element_type=F32)
+            extra += rows[:, cols:]
 
     lane = lax.broadcasted_iota(jnp.int32, extra.shape, 1)
     mine = WEIGHT_LANE + 3 * s_me
@@ -415,9 +464,12 @@
     rows_all = seq * ep
     dma = pltpu.SemaphoreType.DMA
     vmem = pltpu.VMEM
+    cuts = row_cuts(cols)
+    row_parts = [vmem((side, seq, ep, cuts[p + 1] - cuts[p]), BF16) for p in range(3)]
     scratch = [
         vmem((batch, kdim, span), BF16),
-        vmem((chunks, side, side, PAIR, group, kdim), BF16),
+        vmem((batch, group, kdim), BF16),
+        vmem((chunks, side, side, group, PAIR * kdim), BF16),
         vmem((chunks, PAIR, heads), F32),
         vmem((chunks, side - 1, PAIR, heads), F32),
         vmem((chunks, side, PAIR, side * group, lat_dim), BF16),
@@ -433,24 +485,22 @@
         vmem((ep, vdim, cols), BF16),
         vmem((ep, units, cols), BF16),
         vmem((width, 2 * units), BF16),
-        vmem((ep, batch, group * vdim), BF16),
+        vmem((ep, 2, batch // 2, group * vdim), BF16),
         vmem((seq, ep, cols), BF16),
         vmem((seq - 1, ep, cols), BF16),
         vmem((ep, 1, cols), F32),
         vmem((ep, cols), F32),
-        vmem((ep, ep, cols + EXTRA), BF16),
-        vmem((2, side, side, ep // 4, ep, cols + EXTRA), BF16),
-        vmem((2, side, side, ep // 4, ep, cols + EXTRA), BF16),
+        *row_parts, *row_parts,
         vmem((ep, rows_all, units), BF16),
         vmem((seq, ep, cols), BF16),
         vmem((seq - 1, ep, cols), BF16),
         vmem((ep, 1, cols), F32),
         vmem((ep, 1, cols), F32),
         dma((batch,)),
-        dma((chunks + 5,)),
+        dma((chunks + 6,)),
     ]
-    scratch += [dma((chunks,)) for _ in range(12)]
-    scratch += [dma((4,)), dma((4,)), dma((6,)), dma((6,)), dma((4,)), dma((4,)), dma((3,)), dma((3,))]
+    scratch += [dma((chunks,)) for _ in range(14)]
+    scratch += [dma((4,)), dma((4,)), dma((6,)), dma((6,)), dma((6,)), dma((6,)), dma((6,)), dma((6,)), dma((2,)), dma((2,))]
     smem = pl.BlockSpec(memory_space=pltpu.SMEM)
     whole = pl.BlockSpec(memory_space=pltpu.VMEM)
     anywhere = pl.BlockSpec(memory_space=pl.ANY)

time: 98.9 us -> 94 us (0.950)
  Pallas kernels: 97.3 us -> 92.4 us
    pallas_call x1, Pallas kernels: 97.3 us -> 92.4 us  [shards(): pl.pallas_call(functools.partial(decode_kernel, side, ep, 192.0 ** (-0.5)...]
where the time goes in v3:
time: 94 us; the launch traced here: 93.8 us
  Pallas kernels  92.4 us (98%)
  other arithmetic  1.38 us (1%)
    pallas_call x1, Pallas kernels, shards(): pl.pallas_call(functools.partial(decode_kernel, side, ep, 192.0 ** (-0.5)...  92.4 us

profile of v3, /device:TPU:1, one launch (start us, length us, event | category | flops | bytes accessed | tf_op | source)
XLA Modules:
  0.0 93.8 jit_solution(8225608722704587947)
XLA Ops:
  0.0 92.4 %decode.1 = f32[8,1,896]{2,1,0:T(1,128)} custom-call(s32[16]{0:T(128)} %lens.1, s32[1,8]{1,0:T(1,128)} %routes.1, f32[1,8]{1,0:T(1,128)} %route_w.1, bf16[16,576,1024]{2,1,0:T(8,128)(2,1)} %bitcast.4, bf16[16,8,576]{2,1,0:T(8,128)(2,1)} %q.1, bf16[1,512,128]{2,1,0:T(8,128)(2,1)} %upv.1, bf16[1,128,7168]{2,1,0:T(8,128)(2,1)} %outp.1, ...), custom_call_target="tpu_custom_call" | custom-call | tf_op jit(solution)/shard_map/decode/pallas_call | solution.py:507
  92.4 1.4 %convert_element_type.14 = bf16[8,1,896]{2,1,0:T(2,128)(2,1)} convert(f32[8,1,896]{2,1,0:T(1,128)} %decode.1) | non-fusion elementwise | flops 7168 | bytes 43008 | tf_op jit(solution)/shard_map/convert_element_type | solution.py:521

commit v4 on v3

--- a/solution.py
+++ b/solution.py
@@ -75,6 +75,10 @@
     def each(lo, hi, body):
         lax.fori_loop(lo, hi, lambda i, c: (body(i), c)[1], 0)
 
+    def unrolled(lo, hi, body):
+        for i in range(lo, hi):
+            body(i)
+
     def other_seq(d):
         return lax.rem(s_me + d, seq)
 
@@ -90,11 +94,11 @@
             wait()
 
     barrier = pltpu.get_barrier_semaphore()
-    each(1, side, lambda d: pl.semaphore_signal(
+    unrolled(1, side, lambda d: pl.semaphore_signal(
         barrier, inc=1, device_id=(plane(0, lax.rem(x + d, side), y), e_me), device_id_type=MESH))
-    each(1, side, lambda d: pl.semaphore_signal(
+    unrolled(1, side, lambda d: pl.semaphore_signal(
         barrier, inc=1, device_id=(plane(0, x, lax.rem(y + d, side)), e_me), device_id_type=MESH))
-    each(1, ep, lambda d: pl.semaphore_signal(
+    unrolled(1, ep, lambda d: pl.semaphore_signal(
         barrier, inc=1, device_id=(s_me, other_ep(d)), device_id_type=MESH))
 
     load_queries = pltpu.make_async_copy(q, qraw, own_sem.at[chunks + 5])
@@ -160,8 +164,8 @@
         send(down.at[0, :, here], edr.at[e_me], w_s.at[2], w_r.at[2], s_me, e)
 
     far = half // 2
-    each(1, half, spread_values)
-    each(1, ep, spread)
+    unrolled(1, half, spread_values)
+    unrolled(1, ep, spread)
     spread_down(0, 1)
     for hop in range(1, half):
         if hop != far:
@@ -278,7 +282,7 @@
         block = lax.div(lax.broadcasted_iota(jnp.int32, values.shape, 1), vdim)
         values = jnp.where(lax.rem(row, group) == lax.rem(block, half) * 2 + lax.div(block, half), values, 0.0)
         hv[e_me, part] = jnp.sum(values.reshape(rows, group, group * vdim), axis=1).astype(BF16)
-        each(1, ep, lambda d: send(
+        unrolled(1, ep, lambda d: send(
             hv.at[e_me, part], hv.at[e_me, part], h_s.at[part], h_r.at[part], s_me, other_ep(d)))
 
     def first_values():
@@ -321,7 +325,7 @@
     attended = jnp.dot(
         hv[...].astype(F32).reshape(rows_all, group * vdim).astype(BF16), opr[...].reshape(ep * vdim, cols), preferred_element_type=F32)
     r5_own[...] = attended.reshape(seq, ep, cols).astype(BF16)
-    each(1, seq, lambda d: send(
+    unrolled(1, seq, lambda d: send(
         r5_own.at[other_seq(d)], r5.at[d - 1], x_s.at[1], x_r.at[1], other_seq(d), e_me))
     left.append(lambda: drain(r5, x_s.at[1]))
 
@@ -361,10 +365,10 @@
         rows_p[p][third, mine] = row[:, cuts[p]:cuts[p + 1]]
 
         def to_plane(i, p=p, first=first, second=second, third=third, mine=mine):
-            s, e = place(p, lax.rem(first + lax.div(i, side), side), lax.rem(second + lax.rem(i, side), side), third)
+            s, e = place(p, lax.rem(first + i // side, side), lax.rem(second + i % side, side), third)
             send(rows_p[p].at[third, mine], rows_p[p].at[third, mine], p_s.at[p], p_r.at[p], s, e)
 
-        each(1, seq, to_plane)
+        unrolled(1, seq, to_plane)
     for p in range(3):
         first, second, third = here[p]
         drain(rows_p[p].at[0, pl.ds(0, seq - 1)], p_r.at[p])
@@ -419,7 +423,7 @@
     gated = gated * rms
     gate_pre, up_pre = gated[:, :units], gated[:, units:]
     act[e_me] = (gate_pre / (1.0 + jnp.exp(-gate_pre)) * up_pre).astype(BF16)
-    each(1, ep, lambda d: send(act.at[e_me], act.at[e_me], x_s.at[3], x_r.at[3], s_me, other_ep(d)))
+    unrolled(1, ep, lambda d: send(act.at[e_me], act.at[e_me], x_s.at[3], x_r.at[3], s_me, other_ep(d)))
     left.append(lambda: drain(act.at[pl.ds(0, ep - 1)], x_s.at[3]))
 
     own_weights[2].wait()
@@ -428,7 +432,7 @@
     acts = jnp.concatenate([act[e] for e in range(ep)], axis=1)
     result = jnp.dot(acts, edr[...].reshape(ep * units, cols), preferred_element_type=F32) * weight
     r8_own[...] = result.reshape(seq, ep, cols).astype(BF16)
-    each(1, seq, lambda d: send(
+    unrolled(1, seq, lambda d: send(
         r8_own.at[other_seq(d)], r8.at[d - 1], x_s.at[4], x_r.at[4], other_seq(d), e_me))
     left.append(lambda: drain(r8, x_s.at[4]))
 
@@ -439,7 +443,7 @@
     mixed = mixed + hid[...]
     mix_own[...] = mixed.reshape(ep, 1, cols)
     mix_got[e_me] = mix_own[e_me]
-    each(1, ep, lambda d: send(
+    unrolled(1, ep, lambda d: send(
         mix_own.at[other_ep(d)], mix_got.at[e_me], x_s.at[5], x_r.at[5], s_me, other_ep(d)))
     left.append(lambda: drain(mix_got.at[pl.ds(0, ep - 1)], x_s.at[5]))
     drain(mix_got.at[pl.ds(0, ep - 1)], x_r.at[5])

time: 94 us -> 93.6 us (level)
  no operation moved by 1% of the time
where the time goes in v4:
time: 93.6 us; the launch traced here: 93.4 us
  Pallas kernels  92 us (98%)
  other arithmetic  1.38 us (1%)
    pallas_call x1, Pallas kernels, shards(): pl.pallas_call(functools.partial(decode_kernel, side, ep, 192.0 ** (-0.5)...  92 us

profile of v4, /device:TPU:1, one launch (start us, length us, event | category | flops | bytes accessed | tf_op | source)
XLA Modules:
  0.0 93.4 jit_solution(14885023288158759030)
XLA Ops:
  0.0 92.0 %decode.1 = f32[8,1,896]{2,1,0:T(1,128)} custom-call(s32[16]{0:T(128)} %lens.1, s32[1,8]{1,0:T(1,128)} %routes.1, f32[1,8]{1,0:T(1,128)} %route_w.1, bf16[16,576,1024]{2,1,0:T(8,128)(2,1)} %bitcast.4, bf16[16,8,576]{2,1,0:T(8,128)(2,1)} %q.1, bf16[1,512,128]{2,1,0:T(8,128)(2,1)} %upv.1, bf16[1,128,7168]{2,1,0:T(8,128)(2,1)} %outp.1, ...), custom_call_target="tpu_custom_call" | custom-call | tf_op jit(solution)/shard_map/decode/pallas_call | solution.py:511
  92.0 1.4 %convert_element_type.14 = bf16[8,1,896]{2,1,0:T(2,128)(2,1)} convert(f32[8,1,896]{2,1,0:T(1,128)} %decode.1) | non-fusion elementwise | flops 7168 | bytes 43008 | tf_op jit(solution)/shard_map/convert_element_type | solution.py:525
